TPU v7x, 32 devices: a whole 2x2x4 slice. The times are simulated.
32 devices in a mesh: ctx: 4 (over y, x), dp: 8 (over z, core).
Axes of the slice: x: 2, y: 2, z: 4, core: 2. Of those that a mesh axis runs over, the one named last changes fastest.
Arguments:
- queries: bfloat16 [8, 4096, 128], P('dp', 'ctx'), may hold values from -24 to 24
- keys: bfloat16 [8, 4096, 128], P('dp', 'ctx'), may hold values from -24 to 24
- values: bfloat16 [8, 4096, 128], P('dp', 'ctx'), may hold values from -6 to 6
- grad_out: bfloat16 [8, 4096, 128], P('dp', 'ctx'), may hold values from -6 to 6
- gain: float32 [1024], P('dp'), may hold values from 0.1 to 1.9
- doc_start: int32 [1, 4096], replicated, may hold values from 0 to 4095, as said below
- win_start: int32 [1, 4096], replicated, may hold values from 0 to 3968, as said below
Outputs:
- grad_queries: bfloat16 [8, 4096, 128], P('dp', 'ctx')
- grad_keys: bfloat16 [8, 4096, 128], P('dp', 'ctx')
- grad_values: bfloat16 [8, 4096, 128], P('dp', 'ctx')
- grad_gain: float32 [1024], P('dp')
Inputs may be any that keep to these rules, and one draw needn't show every extreme that they name: Documents are contiguous runs of positions: doc_start of a row is at most its position, equals its own position at a document's first row, and is the same for all rows of a document. win_start is a multiple of 128, at most the start of the row's block of 128 positions and at least (7) * 128 positions before that start.
All inputs are finite; a program needn't handle non-finite values.
Results may differ from a plain program's by a relative error of at most 0.012.
The roundings to bfloat16 on the way count: a program that leaves them out, or rounds other values in their place, can miss the bound.
Values may be sent and summed in bfloat16 or wider, within the bound.
No kernel may reach another device: no remote copies, remote signals or barrier semaphores. Data moves between devices by JAX's collectives and lax.ppermute only.
A program may use at most 64 MiB of HBM per device.

v0:
```python
import math

import jax
import jax.numpy as jnp
from jax import lax
from jax.sharding import PartitionSpec as P

HEADS = 8
BLK = 128
WBLK = 8


def from_behind(value, axis, by):
    length = lax.axis_size(axis)
    pairs = [(i, i + by) for i in range(length) if 0 <= i + by < length]
    return lax.ppermute(value, axis, pairs)


def block_scores(left_rows, right_rows):
    return jnp.einsum("bnqd,bnkd->bnqk", left_rows, right_rows, preferred_element_type=jnp.float32)


def block_mix(weights, right_rows):
    return jnp.einsum("bnqk,bnkd->bnqd", weights, right_rows, preferred_element_type=jnp.float32)


def block_back(weights, left_rows):
    return jnp.einsum("bnqk,bnqd->bnkd", weights, left_rows, preferred_element_type=jnp.float32)


def spread(parts, pair_count, group_rows, head_width):
    summed = jnp.zeros((pair_count, (WBLK - 1) * BLK + group_rows, head_width), jnp.float32)
    for offset in range(WBLK):
        slab_rows = parts[offset].reshape(pair_count, group_rows, head_width)
        summed = summed + jnp.pad(
            slab_rows, ((0, 0), (offset * BLK, (WBLK - 1 - offset) * BLK), (0, 0))
        )
    return summed


def band_mask(first_row, lower_bound, nblock):
    query_pos = (first_row + jnp.arange(nblock * BLK, dtype=jnp.int32)).reshape(nblock, BLK)
    key_pos = (
        first_row
        - (WBLK - 1) * BLK
        + (jnp.arange(nblock, dtype=jnp.int32) * BLK)[:, None]
        + jnp.arange(WBLK * BLK, dtype=jnp.int32)[None, :]
    )
    return (key_pos[:, None, :] >= lower_bound.reshape(nblock, BLK)[:, :, None]) & (
        key_pos[:, None, :] <= query_pos[:, :, None]
    )


def band_terms(query_blocks, grad_blocks, key_window, value_window, visible, score_scale):
    pair_count, nblock, blk_rows, head_width = query_blocks.shape
    group_rows = nblock * blk_rows
    key_slabs = [
        key_window[:, offset * blk_rows : offset * blk_rows + group_rows].reshape(
            pair_count, nblock, blk_rows, head_width
        )
        for offset in range(WBLK)
    ]
    value_slabs = [
        value_window[:, offset * blk_rows : offset * blk_rows + group_rows].reshape(
            pair_count, nblock, blk_rows, head_width
        )
        for offset in range(WBLK)
    ]
    slab_shape = (pair_count, nblock, blk_rows, head_width)
    scores = (
        jnp.concatenate(
            [block_scores(query_blocks, key_slabs[offset]) for offset in range(WBLK)], axis=-1
        )
        * score_scale
    )
    scores = jnp.where(visible[None], scores, -jnp.inf)
    weights = jnp.exp(scores - jnp.max(scores, axis=-1, keepdims=True))
    attn_probs = (weights / jnp.sum(weights, axis=-1, keepdims=True)).astype(jnp.bfloat16)
    prob_grad = jnp.concatenate(
        [block_scores(grad_blocks, value_slabs[offset]) for offset in range(WBLK)], axis=-1
    )
    row_delta = jnp.sum(attn_probs.astype(jnp.float32) * prob_grad, axis=-1, keepdims=True)
    score_grad = (attn_probs.astype(jnp.float32) * (prob_grad - row_delta)).astype(jnp.bfloat16)
    mixed = jnp.zeros(slab_shape, jnp.float32)
    key_parts = []
    value_parts = []
    for offset in range(WBLK):
        score_slab = score_grad[..., offset * blk_rows : (offset + 1) * blk_rows]
        prob_slab = attn_probs[..., offset * blk_rows : (offset + 1) * blk_rows]
        mixed = mixed + block_mix(score_slab, key_slabs[offset])
        key_parts.append(block_back(score_slab, query_blocks) * score_scale)
        value_parts.append(block_back(prob_slab, grad_blocks))
    return (
        mixed * score_scale,
        spread(key_parts, pair_count, group_rows, head_width),
        spread(value_parts, pair_count, group_rows, head_width),
    )


def on_device(queries, keys, values, grad_out, gain, doc_start, win_start):
    pair_count, tok_rows, head_width = queries.shape
    nblock = tok_rows // BLK
    group_blocks = math.gcd(nblock, max(1, 512 // BLK))
    group_rows = group_blocks * BLK
    prev_rows = (WBLK - 1) * BLK
    span_rows = prev_rows + group_rows
    score_scale = 1.0 / math.sqrt(head_width)
    first_row = lax.axis_index("ctx") * tok_rows
    first_pair = lax.axis_index("dp") * pair_count
    head_first = first_pair % HEADS
    seq_index = first_pair // HEADS
    full_gain = lax.all_gather(gain, "dp", axis=0, tiled=True)
    gain_rows = lax.dynamic_slice_in_dim(
        full_gain.reshape(HEADS, head_width), head_first, pair_count, 0
    )
    scaled = (queries.astype(jnp.float32) * gain_rows[:, None, :]).astype(jnp.bfloat16)
    earlier = from_behind(
        (keys[:, tok_rows - prev_rows :], values[:, tok_rows - prev_rows :]), "ctx", 1
    )
    key_ext = jnp.concatenate([earlier[0], keys], axis=1)
    value_ext = jnp.concatenate([earlier[1], values], axis=1)
    seq_docs = lax.dynamic_index_in_dim(doc_start, seq_index, 0, keepdims=False)
    seq_wins = lax.dynamic_index_in_dim(win_start, seq_index, 0, keepdims=False)
    lower_full = jnp.maximum(seq_docs, seq_wins)
    lower_bound = lax.dynamic_slice_in_dim(lower_full, first_row, tok_rows, 0)
    visible = band_mask(first_row, lower_bound, nblock)
    query_blocks = scaled.reshape(pair_count, nblock, BLK, head_width)
    grad_blocks = grad_out.reshape(pair_count, nblock, BLK, head_width)

    def group_step(group_index, state_tuple):
        grad_scaled, key_grad, value_grad = state_tuple
        block_first = group_index * group_blocks
        row_first = block_first * BLK
        grad_piece, key_piece, value_piece = band_terms(
            lax.dynamic_slice_in_dim(query_blocks, block_first, group_blocks, 1),
            lax.dynamic_slice_in_dim(grad_blocks, block_first, group_blocks, 1),
            lax.dynamic_slice_in_dim(key_ext, row_first, span_rows, 1),
            lax.dynamic_slice_in_dim(value_ext, row_first, span_rows, 1),
            lax.dynamic_slice_in_dim(visible, block_first, group_blocks, 0),
            score_scale,
        )
        grad_scaled = lax.dynamic_update_slice_in_dim(grad_scaled, grad_piece, block_first, 1)
        key_grad = lax.dynamic_update_slice_in_dim(
            key_grad,
            lax.dynamic_slice_in_dim(key_grad, row_first, span_rows, 1) + key_piece,
            row_first,
            1,
        )
        value_grad = lax.dynamic_update_slice_in_dim(
            value_grad,
            lax.dynamic_slice_in_dim(value_grad, row_first, span_rows, 1) + value_piece,
            row_first,
            1,
        )
        return (grad_scaled, key_grad, value_grad)

    initial = (
        jnp.zeros((pair_count, nblock, BLK, head_width), jnp.float32),
        jnp.zeros((pair_count, prev_rows + tok_rows, head_width), jnp.float32),
        jnp.zeros((pair_count, prev_rows + tok_rows, head_width), jnp.float32),
    )
    grad_scaled, key_ext_grad, value_ext_grad = lax.fori_loop(
        0, nblock // group_blocks, group_step, initial
    )
    grad_scaled = grad_scaled.reshape(pair_count, tok_rows, head_width)
    key_own = key_ext_grad[:, prev_rows:]
    value_own = value_ext_grad[:, prev_rows:]
    returned = from_behind(
        (
            key_ext_grad[:, :prev_rows].astype(jnp.bfloat16),
            value_ext_grad[:, :prev_rows].astype(jnp.bfloat16),
        ),
        "ctx",
        -1,
    )
    key_own = key_own.at[:, tok_rows - prev_rows :].add(returned[0].astype(jnp.float32))
    value_own = value_own.at[:, tok_rows - prev_rows :].add(returned[1].astype(jnp.float32))
    grad_queries = (grad_scaled * gain_rows[:, None, :]).astype(jnp.bfloat16)
    head_terms = jnp.sum(grad_scaled * queries.astype(jnp.float32), axis=1)
    gain_table = lax.dynamic_update_slice_in_dim(
        jnp.zeros((HEADS, head_width), jnp.float32), head_terms, head_first, 0
    ).reshape(HEADS * head_width)
    everything = lax.psum(gain_table, ("ctx", "dp"))
    share_len = everything.shape[0] // lax.axis_size("dp")
    grad_gain = lax.dynamic_slice_in_dim(everything, lax.axis_index("dp") * share_len, share_len, 0)
    return (grad_queries, key_own.astype(jnp.bfloat16), value_own.astype(jnp.bfloat16), grad_gain)


def solution(mesh):
    placed = (
        P("dp", "ctx", None),
        P("dp", "ctx", None),
        P("dp", "ctx", None),
        P("dp", "ctx", None),
        P("dp"),
        P(),
        P(),
    )
    return jax.shard_map(
        on_device,
        mesh=mesh,
        in_specs=placed,
        out_specs=(P("dp", "ctx", None), P("dp", "ctx", None), P("dp", "ctx", None), P("dp")),
        check_vma=False,
    )
```

profile of v0, /device:TPU:0, one launch (start us, length us, event | category | flops | bytes accessed | tf_op | source)
XLA Modules:
  0.0 116.2 jit_solution(16396689492414739092)
XLA Ops:
  0.7 1.0 slice.390
  1.7 4.9 %collective-permute-start = (bf16[1,896,128]{2,1,0:T(8,128)(2,1)S(1)}, bf16[1,896,128]{2,1,0:T(8,128)(2,1)S(1)}, u32[]{:S(2)}, u32[]{:S(2)}) collective-permute-start(bf16[1,896,128]{2,1,0:T(8,128)(2,1)S(1)} %slice.390), channel_id=1, source_target_pairs={{0,8},{8,16},{16,24},{1,9},{9,17},{17,25},{2,10},{10,18},{18,26},{... | collective-permute-start | bytes 688136 | tf_op jit(solution)/shard_map/ppermute | solution.py:16
  6.6 1.0 slice.391
  7.5 3.4 %collective-permute-start.1 = (bf16[1,896,128]{2,1,0:T(8,128)(2,1)S(1)}, bf16[1,896,128]{2,1,0:T(8,128)(2,1)S(1)}, u32[]{:S(2)}, u32[]{:S(2)}) collective-permute-start(bf16[1,896,128]{2,1,0:T(8,128)(2,1)S(1)} %slice.391), channel_id=1, source_target_pairs={{0,8},{8,16},{16,24},{1,9},{9,17},{17,25},{2,10},{10,18},{18,26},{... | collective-permute-start | bytes 688136 | tf_op jit(solution)/shard_map/ppermute | solution.py:16
  11.0 12.1 %all-gather = f32[8,1,128]{2,1,0:T(1,128)S(1)} all-gather(f32[1,1,128]{2,1,0:T(1,128)} %bitcast.481), channel_id=1, replica_groups=mesh['ctx'=4,'dp'=8] {'dp'}, dimensions={0}, use_global_device_ids=true | all-gather | bytes 4608 | tf_op jit(solution)/shard_map/all_gather | solution.py:112
  23.1 0.7 dynamic-slice_maximum_fusion
  23.8 3.4 %compare_and_fusion = pred[8,128,1024]{1,2,0:T(8,128)(4,1)} fusion(s32[8,128]{1,0:T(8,128)S(1)} %add_add_fusion, s32[8,128]{1,0:T(8,128)S(1)} %bitcast.478, s32[8,1024]{1,0:T(8,128)S(1)} %iota_add_fusion), kind=kLoop, calls=%fused_computation.131 | loop fusion | flops 3145728 | bytes 1089536 | tf_op jit(solution)/shard_map/and | solution.py:49
  27.5 0.8 broadcast_in_dim.30
  28.4 1.0 broadcast.201.clone
  29.4 34.3 %while.21 = (s32[]{:T(128)}, f32[1,8,128,128]{3,2,1,0:T(8,128)}, f32[1,1920,128]{2,1,0:T(8,128)S(1)}, f32[1,1920,128]{2,1,0:T(8,128)}, pred[8,128,1024]{1,2,0:T(...) while((s32[]{:T(128)}, f32[1,8,128,128]{3,2,1,0:T(8,128)}, ...), condition=%wide.region_4.5_spmd, body=%wide.region_0.4_spmd.sunk | while | flops 680792576 | bytes 79168672 | solution.py:162
  33.3 1.3 %copy-done.27 = f32[4,128,1024]{1,2,0:T(8,128)} copy-done((f32[4,128,1024]{1,2,0:T(8,128)}, f32[4,128,1024]{1,2,0:T(8,128)S(1)}, u32[]{:S(2)}) %copy-start.27) | copy-done | bytes 2097176 | tf_op jit(solution)/shard_map/while
  34.6 2.5 %divide_convert_fusion.2 = bf16[4,128,1024]{1,2,0:T(8,128)(2,1)S(1)} fusion(f32[4,128,1024]{1,2,0:T(8,128)} %copy-done.27, pred[8,128,1024]{1,2,0:T(8,128)(4,1)} %get-tuple-element.431, s32[]{:T(128)S(6)} %select_n.76), kind=kOutput, calls=%fused_computation.6.clone.1 | output fusion | flops 2624510 | bytes 3670020 | tf_op jit(solution)/shard_map/while/body/eval_jaxpr/div | solution.py:78
  37.1 2.9 %fusion.213 = bf16[1,4,128,1024]{2,3,1,0:T(8,128)(2,1)S(1)} fusion(f32[4,128,1024]{1,2,0:T(8,128)} %copy-done.1, bf16[4,128,1024]{1,2,0:T(8,128)(2,1)S(1)} %divide_convert_fusion.2), kind=kOutput, calls=%fused_computation.11.clone.1 | output fusion | flops 3147263 | bytes 4194304 | tf_op jit(solution)/shard_map/while/body/eval_jaxpr/sub | solution.py:83
  40.3 0.2 convolution_add_fusion.13
  41.9 0.2 fusion.215
  45.2 0.4 add_dynamic-update-slice_fusion.5
  45.6 1.0 copy-done.3
  50.4 1.3 %copy-done.27 = f32[4,128,1024]{1,2,0:T(8,128)} copy-done((f32[4,128,1024]{1,2,0:T(8,128)}, f32[4,128,1024]{1,2,0:T(8,128)S(1)}, u32[]{:S(2)}) %copy-start.27) | copy-done | bytes 2097176 | tf_op jit(solution)/shard_map/while
  51.7 2.5 %divide_convert_fusion.2 = bf16[4,128,1024]{1,2,0:T(8,128)(2,1)S(1)} fusion(f32[4,128,1024]{1,2,0:T(8,128)} %copy-done.27, pred[8,128,1024]{1,2,0:T(8,128)(4,1)} %get-tuple-element.431, s32[]{:T(128)S(6)} %select_n.76), kind=kOutput, calls=%fused_computation.6.clone.1 | output fusion | flops 2624510 | bytes 3670020 | tf_op jit(solution)/shard_map/while/body/eval_jaxpr/div | solution.py:78
  54.2 2.9 %fusion.213 = bf16[1,4,128,1024]{2,3,1,0:T(8,128)(2,1)S(1)} fusion(f32[4,128,1024]{1,2,0:T(8,128)} %copy-done.1, bf16[4,128,1024]{1,2,0:T(8,128)(2,1)S(1)} %divide_convert_fusion.2), kind=kOutput, calls=%fused_computation.11.clone.1 | output fusion | flops 3147263 | bytes 4194304 | tf_op jit(solution)/shard_map/while/body/eval_jaxpr/sub | solution.py:83
  59.1 0.2 fusion.215
  62.3 0.4 add_dynamic-update-slice_fusion.5
  62.7 1.0 copy-done.3
  63.8 1.1 slice.395
  64.9 1.0 slice.460
  66.0 1.3 %collective-permute-start.2 = (bf16[1,896,128]{2,1,0:T(8,128)(2,1)S(1)}, bf16[1,896,128]{2,1,0:T(8,128)(2,1)S(1)}, u32[]{:S(2)}, u32[]{:S(2)}) collective-permute-start(bf16[1,896,128]{2,1,0:T(8,128)(2,1)S(1)} %slice.461), channel_id=1, source_target_pairs={{8,0},{16,8},{24,16},{9,1},{17,9},{25,17},{10,2},{18,10},{26,18},{... | collective-permute-start | bytes 688136 | tf_op jit(solution)/shard_map/ppermute | solution.py:16
  67.3 1.3 %collective-permute-start.3 = (bf16[1,896,128]{2,1,0:T(8,128)(2,1)S(1)}, bf16[1,896,128]{2,1,0:T(8,128)(2,1)S(1)}, u32[]{:S(2)}, u32[]{:S(2)}) collective-permute-start(bf16[1,896,128]{2,1,0:T(8,128)(2,1)S(1)} %slice.460), channel_id=1, source_target_pairs={{8,0},{16,8},{24,16},{9,1},{17,9},{25,17},{10,2},{18,10},{26,18},{... | collective-permute-start | bytes 688136 | tf_op jit(solution)/shard_map/ppermute | solution.py:16
  68.6 0.8 fusion.63
  69.4 44.3 %psum.7 = f32[1024]{0:T(1024)S(1)} all-reduce(f32[1024]{0:T(1024)S(1)} %bitcast.479), channel_id=1, replica_groups=mesh['ctx'=4,'dp'=8] {'ctx','dp'}, use_global_device_ids=true, to_apply=%region_6.7 | all-reduce | flops 1024 | bytes 8192 | tf_op jit(solution)/shard_map/psum | solution.py:183
  113.7 0.6 dynamic_slice.84
  114.4 1.2 %add_dynamic-update-slice_fusion.2 = bf16[1,1024,128]{2,1,0:T(8,128)(2,1)S(1)} fusion(bf16[1,1024,128]{2,1,0:T(8,128)(2,1)S(1)} %slice.395, bf16[1,896,128]{2,1,0:T(8,128)(2,1)S(1)} %collective-permute-done.3, f32[1,1920,128]{2,1,0:T(8,128)} %get-tuple-element.253), kind=kLoop, calls=%fused_computation.142 | loop fusion | flops 229376 | bytes 1146880 | tf_op jit(solution)/shard_map/scatter-add | solution.py:177
  115.6 0.7 copy-done.28
  (197 shorter events, 16.7 us)
Async XLA Ops:
  0.6 26.7 %copy-start.25 = (bf16[1,1024,128]{2,1,0:T(8,128)(2,1)S(1)}, bf16[1,1024,128]{2,1,0:T(8,128)(2,1)}, u32[]{:S(2)}) copy-start(bf16[1,1024,128]{2,1,0:T(8,128)(2,1)} %param.14) | copy-start | bytes 786436
  0.6 26.8 %copy-start.26 = (bf16[1,1024,128]{2,1,0:T(8,128)(2,1)S(1)}, bf16[1,1024,128]{2,1,0:T(8,128)(2,1)}, u32[]{:S(2)}) copy-start(bf16[1,1024,128]{2,1,0:T(8,128)(2,1)} %param.15) | copy-start | bytes 786436
  0.7 26.6 %copy-start.23 = (bf16[1,1024,128]{2,1,0:T(8,128)(2,1)S(1)}, bf16[1,1024,128]{2,1,0:T(8,128)(2,1)}, u32[]{:S(2)}) copy-start(bf16[1,1024,128]{2,1,0:T(8,128)(2,1)} %param.13) | copy-start | bytes 786436
  1.7 25.7 %collective-permute-start = (bf16[1,896,128]{2,1,0:T(8,128)(2,1)S(1)}, bf16[1,896,128]{2,1,0:T(8,128)(2,1)S(1)}, u32[]{:S(2)}, u32[]{:S(2)}) collective-permute-start(bf16[1,896,128]{2,1,0:T(8,128)(2,1)S(1)} %slice.390), channel_id=1, source_target_pairs={{0,8},{8,16},{16,24},{1,9},{9,17},{17,25},{2,10},{10,18},{18,26},{... | collective-permute-start | bytes 688136 | tf_op jit(solution)/shard_map/ppermute | solution.py:16
  7.5 19.9 %collective-permute-start.1 = (bf16[1,896,128]{2,1,0:T(8,128)(2,1)S(1)}, bf16[1,896,128]{2,1,0:T(8,128)(2,1)S(1)}, u32[]{:S(2)}, u32[]{:S(2)}) collective-permute-start(bf16[1,896,128]{2,1,0:T(8,128)(2,1)S(1)} %slice.391), channel_id=1, source_target_pairs={{0,8},{8,16},{16,24},{1,9},{9,17},{17,25},{2,10},{10,18},{18,26},{... | collective-permute-start | bytes 688136 | tf_op jit(solution)/shard_map/ppermute | solution.py:16
  27.3 2.1 %copy-start = (bf16[1,1024,128]{2,1,0:T(8,128)(2,1)S(1)}, bf16[1,1024,128]{2,1,0:T(8,128)(2,1)}, u32[]{:S(2)}) copy-start(bf16[1,1024,128]{2,1,0:T(8,128)(2,1)} %param.16) | copy-start | bytes 786436
  29.5 1.9 %copy-start.18 = (bf16[1,512,128]{2,1,0:T(8,128)(2,1)}, bf16[1,512,128]{2,1,0:T(8,128)(2,1)S(1)}, u32[]{:S(2)}) copy-start(bf16[1,512,128]{2,1,0:T(8,128)(2,1)S(1)} %get-tuple-element.365) | copy-start | bytes 393220 | tf_op jit(solution)/shard_map/while
  29.5 2.2 %copy-start.16 = (bf16[1,512,128]{2,1,0:T(8,128)(2,1)}, bf16[1,512,128]{2,1,0:T(8,128)(2,1)S(1)}, u32[]{:S(2)}) copy-start(bf16[1,512,128]{2,1,0:T(8,128)(2,1)S(1)} %get-tuple-element.374) | copy-start | bytes 393220 | tf_op jit(solution)/shard_map/while
  29.5 2.4 %copy-start.14 = (bf16[1,512,128]{2,1,0:T(8,128)(2,1)}, bf16[1,512,128]{2,1,0:T(8,128)(2,1)S(1)}, u32[]{:S(2)}) copy-start(bf16[1,512,128]{2,1,0:T(8,128)(2,1)S(1)} %get-tuple-element.375) | copy-start | bytes 393220 | tf_op jit(solution)/shard_map/while
  29.6 2.6 %copy-start.12 = (bf16[1,512,128]{2,1,0:T(8,128)(2,1)}, bf16[1,512,128]{2,1,0:T(8,128)(2,1)S(1)}, u32[]{:S(2)}) copy-start(bf16[1,512,128]{2,1,0:T(8,128)(2,1)S(1)} %get-tuple-element.376) | copy-start | bytes 393220 | tf_op jit(solution)/shard_map/while
  29.6 2.8 %copy-start.10 = (bf16[1,512,128]{2,1,0:T(8,128)(2,1)}, bf16[1,512,128]{2,1,0:T(8,128)(2,1)S(1)}, u32[]{:S(2)}) copy-start(bf16[1,512,128]{2,1,0:T(8,128)(2,1)S(1)} %get-tuple-element.377) | copy-start | bytes 393220 | tf_op jit(solution)/shard_map/while
  29.6 3.0 %copy-start.8 = (bf16[1,512,128]{2,1,0:T(8,128)(2,1)}, bf16[1,512,128]{2,1,0:T(8,128)(2,1)S(1)}, u32[]{:S(2)}) copy-start(bf16[1,512,128]{2,1,0:T(8,128)(2,1)S(1)} %get-tuple-element.378) | copy-start | bytes 393220 | tf_op jit(solution)/shard_map/while
  29.6 3.2 %copy-start.6 = (bf16[1,512,128]{2,1,0:T(8,128)(2,1)}, bf16[1,512,128]{2,1,0:T(8,128)(2,1)S(1)}, u32[]{:S(2)}) copy-start(bf16[1,512,128]{2,1,0:T(8,128)(2,1)S(1)} %get-tuple-element.379) | copy-start | bytes 393220 | tf_op jit(solution)/shard_map/while
  29.6 3.5 %copy-start.4 = (bf16[1,512,128]{2,1,0:T(8,128)(2,1)}, bf16[1,512,128]{2,1,0:T(8,128)(2,1)S(1)}, u32[]{:S(2)}) copy-start(bf16[1,512,128]{2,1,0:T(8,128)(2,1)S(1)} %get-tuple-element.380) | copy-start | bytes 393220 | tf_op jit(solution)/shard_map/while
  37.1 2.9 %copy-start.19 = (bf16[1,512,128]{2,1,0:T(8,128)(2,1)S(1)}, bf16[1,512,128]{2,1,0:T(8,128)(2,1)}, u32[]{:S(2)}) copy-start(bf16[1,512,128]{2,1,0:T(8,128)(2,1)} %copy-done.18) | copy-start | bytes 393220 | tf_op jit(solution)/shard_map/while
  37.1 3.2 %copy-start.17 = (bf16[1,512,128]{2,1,0:T(8,128)(2,1)S(1)}, bf16[1,512,128]{2,1,0:T(8,128)(2,1)}, u32[]{:S(2)}) copy-start(bf16[1,512,128]{2,1,0:T(8,128)(2,1)} %copy-done.16) | copy-start | bytes 393220 | tf_op jit(solution)/shard_map/while
  37.1 3.4 %copy-start.15 = (bf16[1,512,128]{2,1,0:T(8,128)(2,1)S(1)}, bf16[1,512,128]{2,1,0:T(8,128)(2,1)}, u32[]{:S(2)}) copy-start(bf16[1,512,128]{2,1,0:T(8,128)(2,1)} %copy-done.14) | copy-start | bytes 393220 | tf_op jit(solution)/shard_map/while
  46.7 1.9 %copy-start.18 = (bf16[1,512,128]{2,1,0:T(8,128)(2,1)}, bf16[1,512,128]{2,1,0:T(8,128)(2,1)S(1)}, u32[]{:S(2)}) copy-start(bf16[1,512,128]{2,1,0:T(8,128)(2,1)S(1)} %get-tuple-element.365) | copy-start | bytes 393220 | tf_op jit(solution)/shard_map/while
  46.7 2.2 %copy-start.16 = (bf16[1,512,128]{2,1,0:T(8,128)(2,1)}, bf16[1,512,128]{2,1,0:T(8,128)(2,1)S(1)}, u32[]{:S(2)}) copy-start(bf16[1,512,128]{2,1,0:T(8,128)(2,1)S(1)} %get-tuple-element.374) | copy-start | bytes 393220 | tf_op jit(solution)/shard_map/while
  46.7 2.4 %copy-start.14 = (bf16[1,512,128]{2,1,0:T(8,128)(2,1)}, bf16[1,512,128]{2,1,0:T(8,128)(2,1)S(1)}, u32[]{:S(2)}) copy-start(bf16[1,512,128]{2,1,0:T(8,128)(2,1)S(1)} %get-tuple-element.375) | copy-start | bytes 393220 | tf_op jit(solution)/shard_map/while
  46.7 2.6 %copy-start.12 = (bf16[1,512,128]{2,1,0:T(8,128)(2,1)}, bf16[1,512,128]{2,1,0:T(8,128)(2,1)S(1)}, u32[]{:S(2)}) copy-start(bf16[1,512,128]{2,1,0:T(8,128)(2,1)S(1)} %get-tuple-element.376) | copy-start | bytes 393220 | tf_op jit(solution)/shard_map/while
  46.7 2.8 %copy-start.10 = (bf16[1,512,128]{2,1,0:T(8,128)(2,1)}, bf16[1,512,128]{2,1,0:T(8,128)(2,1)S(1)}, u32[]{:S(2)}) copy-start(bf16[1,512,128]{2,1,0:T(8,128)(2,1)S(1)} %get-tuple-element.377) | copy-start | bytes 393220 | tf_op jit(solution)/shard_map/while
  46.7 3.0 %copy-start.8 = (bf16[1,512,128]{2,1,0:T(8,128)(2,1)}, bf16[1,512,128]{2,1,0:T(8,128)(2,1)S(1)}, u32[]{:S(2)}) copy-start(bf16[1,512,128]{2,1,0:T(8,128)(2,1)S(1)} %get-tuple-element.378) | copy-start | bytes 393220 | tf_op jit(solution)/shard_map/while
  46.7 3.2 %copy-start.6 = (bf16[1,512,128]{2,1,0:T(8,128)(2,1)}, bf16[1,512,128]{2,1,0:T(8,128)(2,1)S(1)}, u32[]{:S(2)}) copy-start(bf16[1,512,128]{2,1,0:T(8,128)(2,1)S(1)} %get-tuple-element.379) | copy-start | bytes 393220 | tf_op jit(solution)/shard_map/while
  46.7 3.5 %copy-start.4 = (bf16[1,512,128]{2,1,0:T(8,128)(2,1)}, bf16[1,512,128]{2,1,0:T(8,128)(2,1)S(1)}, u32[]{:S(2)}) copy-start(bf16[1,512,128]{2,1,0:T(8,128)(2,1)S(1)} %get-tuple-element.380) | copy-start | bytes 393220 | tf_op jit(solution)/shard_map/while
  54.2 2.9 %copy-start.19 = (bf16[1,512,128]{2,1,0:T(8,128)(2,1)S(1)}, bf16[1,512,128]{2,1,0:T(8,128)(2,1)}, u32[]{:S(2)}) copy-start(bf16[1,512,128]{2,1,0:T(8,128)(2,1)} %copy-done.18) | copy-start | bytes 393220 | tf_op jit(solution)/shard_map/while
  54.2 3.2 %copy-start.17 = (bf16[1,512,128]{2,1,0:T(8,128)(2,1)S(1)}, bf16[1,512,128]{2,1,0:T(8,128)(2,1)}, u32[]{:S(2)}) copy-start(bf16[1,512,128]{2,1,0:T(8,128)(2,1)} %copy-done.16) | copy-start | bytes 393220 | tf_op jit(solution)/shard_map/while
  54.2 3.4 %copy-start.15 = (bf16[1,512,128]{2,1,0:T(8,128)(2,1)S(1)}, bf16[1,512,128]{2,1,0:T(8,128)(2,1)}, u32[]{:S(2)}) copy-start(bf16[1,512,128]{2,1,0:T(8,128)(2,1)} %copy-done.14) | copy-start | bytes 393220 | tf_op jit(solution)/shard_map/while
  63.7 4.8 %copy-start.22 = (f32[1,8,128,128]{3,2,1,0:T(8,128)S(1)}, f32[1,8,128,128]{3,2,1,0:T(8,128)}, u32[]{:S(2)}) copy-start(f32[1,8,128,128]{3,2,1,0:T(8,128)} %get-tuple-element.251) | copy-start | bytes 1572868
  63.7 4.9 %copy-start.24 = (bf16[1,1024,128]{2,1,0:T(8,128)(2,1)S(1)}, bf16[1,1024,128]{2,1,0:T(8,128)(2,1)}, u32[]{:S(2)}) copy-start(bf16[1,1024,128]{2,1,0:T(8,128)(2,1)} %param.13) | copy-start | bytes 786436
  66.0 48.3 %collective-permute-start.2 = (bf16[1,896,128]{2,1,0:T(8,128)(2,1)S(1)}, bf16[1,896,128]{2,1,0:T(8,128)(2,1)S(1)}, u32[]{:S(2)}, u32[]{:S(2)}) collective-permute-start(bf16[1,896,128]{2,1,0:T(8,128)(2,1)S(1)} %slice.461), channel_id=1, source_target_pairs={{8,0},{16,8},{24,16},{9,1},{17,9},{25,17},{10,2},{18,10},{26,18},{... | collective-permute-start | bytes 688136 | tf_op jit(solution)/shard_map/ppermute | solution.py:16
  67.3 47.1 %collective-permute-start.3 = (bf16[1,896,128]{2,1,0:T(8,128)(2,1)S(1)}, bf16[1,896,128]{2,1,0:T(8,128)(2,1)S(1)}, u32[]{:S(2)}, u32[]{:S(2)}) collective-permute-start(bf16[1,896,128]{2,1,0:T(8,128)(2,1)S(1)} %slice.460), channel_id=1, source_target_pairs={{8,0},{16,8},{24,16},{9,1},{17,9},{25,17},{10,2},{18,10},{26,18},{... | collective-permute-start | bytes 688136 | tf_op jit(solution)/shard_map/ppermute | solution.py:16
  (24 other events, 31.2 us)
where the time goes:
time: 117 us; the launch traced here: 116 us
  blocking collectives  56.4 us (48%)
  other arithmetic  17.9 us (15%)
  matrix products  16.2 us (14%)
  local copies, waits for them, and re-layouts  12.8 us (11%)
  starting transfers between devices  10.8 us (9%)
  loops' own time  1.26 us (1%)
    psum x1, blocking collectives, on_device(): everything = lax.psum(gain_table, ('ctx', 'dp'))  44.3 us
    all_gather x1, blocking collectives, on_device(): full_gain = lax.all_gather(gain, 'dp', axis=0, tiled=True)  12.1 us
    ppermute x4, starting transfers between devices, from_behind(): return lax.ppermute(value, axis, pairs)  10.8 us
    dot_general x32, matrix products, block_scores(): jnp.einsum('bnqd,bnkd->bnqk', left_rows, right_rows, preferred_element_ty...  6.77 us
    sub x2, other arithmetic, band_terms(): prob_grad - row_delta  5.76 us
    dot_general x32, matrix products, block_back(): jnp.einsum('bnqk,bnqd->bnkd', weights, left_rows, preferred_element_type=...  5.7 us
    while x88, local copies, waits for them, and re-layouts  4.93 us
    div x2, other arithmetic, band_terms(): weights / jnp.sum(weights, axis=-1, keepdims=True)  4.93 us
  transfers between devices with their start and end apart: 4, of which 0 were waited for; matrix products, arithmetic and copies ran while one was open for 6% of the time, Pallas kernels for 0%

commit v1 on v0

v1 whole, which is shorter than its diff:
```python
import functools
import math

import jax
import jax.numpy as jnp
from jax import lax
from jax.experimental import pallas as pl
from jax.experimental.pallas import tpu as pltpu
from jax.sharding import PartitionSpec as P

HEADS = 8
BLK = 128
WBLK = 8
PREV = (WBLK - 1) * BLK
GROUP = 2 * BLK
LOG2E = 1.4426950408889634
NEG = -1e30
M_ROW, L_ROW, D_ROW = 0, 1, 2


def shift(value, axis, by):
    length = lax.axis_size(axis)
    pairs = [(i, (i + by) % length) for i in range(length)]
    return lax.ppermute(value, axis, pairs)


def mm(left, right):
    return lax.dot_general(left, right, (((1,), (0,)), ((), ())), preferred_element_type=jnp.float32)


def mm_t(left, right):
    return lax.dot_general(left, right, (((1,), (1,)), ((), ())), preferred_element_type=jnp.float32)


def scaled_rows(q_ref, gain_ref, start, width):
    rows = q_ref[0, start : start + width, :].astype(jnp.float32) * gain_ref[0]
    return rows.astype(jnp.bfloat16)


def own_logits(k_ref, scaled, low_ref, start, width, factor):
    stop = start + width
    logits = mm_t(k_ref[0, :stop, :], scaled) * factor
    key_at = lax.broadcasted_iota(jnp.int32, (stop, width), 0)
    query_at = start + lax.broadcasted_iota(jnp.int32, (stop, width), 1)
    visible = (key_at >= low_ref[:, start:stop]) & (key_at <= query_at)
    return jnp.where(visible, logits, NEG)


def stats_kernel(q_ref, k_ref, v_ref, g_ref, gain_ref, low_ref, stats_ref, *, factor):
    rows = q_ref.shape[1]
    for start in range(0, rows, GROUP):
        width = min(GROUP, rows - start)
        stop = start + width
        scaled = scaled_rows(q_ref, gain_ref, start, width)
        logits = own_logits(k_ref, scaled, low_ref, start, width, factor)
        top = jnp.max(logits, axis=0, keepdims=True)
        weights = jnp.exp2(logits - top)
        prob_grad = mm_t(v_ref[0, :stop, :], g_ref[0, start:stop, :])
        stats_ref[0, M_ROW : M_ROW + 1, start:stop] = top
        stats_ref[0, L_ROW : L_ROW + 1, start:stop] = jnp.sum(weights, axis=0, keepdims=True)
        stats_ref[0, D_ROW : D_ROW + 1, start:stop] = jnp.sum(weights * prob_grad, axis=0, keepdims=True)


def halo_kernel(
    q_ref, g_ref, gain_ref, low_ref, part_ref, kv_ref,
    stats_ref, dq_ref, dkv_ref, probs_ref, grads_ref, *, factor, score_scale,
):
    rows = q_ref.shape[1]
    key_cols = kv_ref[0, 0].T
    for start in range(0, PREV, GROUP):
        width = min(GROUP, PREV - start)
        stop = start + width
        scaled = scaled_rows(q_ref, gain_ref, start, width)
        logits = mm_t(kv_ref[0, 0, start:, :], scaled) * factor
        key_at = (start - PREV) + lax.broadcasted_iota(jnp.int32, (PREV - start, width), 0)
        logits = jnp.where(key_at >= low_ref[:, start:stop], logits, NEG)
        own_top = part_ref[0, M_ROW : M_ROW + 1, start:stop]
        top = jnp.maximum(own_top, jnp.max(logits, axis=0, keepdims=True))
        weights = jnp.exp2(logits - top)
        prob_grad = mm_t(kv_ref[1, 0, start:, :], g_ref[0, start:stop, :])
        shrink = jnp.exp2(own_top - top)
        total = part_ref[0, L_ROW : L_ROW + 1, start:stop] * shrink + jnp.sum(weights, axis=0, keepdims=True)
        inverse = 1.0 / total
        delta = (
            part_ref[0, D_ROW : D_ROW + 1, start:stop] * shrink
            + jnp.sum(weights * prob_grad, axis=0, keepdims=True)
        ) * inverse
        stats_ref[0, M_ROW : M_ROW + 1, start:stop] = top
        stats_ref[0, L_ROW : L_ROW + 1, start:stop] = inverse
        stats_ref[0, D_ROW : D_ROW + 1, start:stop] = delta
        probs = (weights * inverse).astype(jnp.bfloat16)
        grads = (probs.astype(jnp.float32) * (prob_grad - delta)).astype(jnp.bfloat16)
        probs_ref[start:, start:stop] = probs
        grads_ref[start:, start:stop] = grads
        dq_ref[0, start:stop, :] = mm(key_cols[:, start:], grads).T
    for start in range(PREV, rows, BLK):
        stop = start + BLK
        inverse = 1.0 / part_ref[0, L_ROW : L_ROW + 1, start:stop]
        stats_ref[0, M_ROW : M_ROW + 1, start:stop] = part_ref[0, M_ROW : M_ROW + 1, start:stop]
        stats_ref[0, L_ROW : L_ROW + 1, start:stop] = inverse
        stats_ref[0, D_ROW : D_ROW + 1, start:stop] = part_ref[0, D_ROW : D_ROW + 1, start:stop] * inverse
    for first in range(0, PREV, GROUP):
        last = min(first + GROUP, PREV)
        all_scaled = scaled_rows(q_ref, gain_ref, 0, last)
        dkv_ref[0, 0, first:last, :] = (mm(grads_ref[first:last, :last], all_scaled) * score_scale).astype(
            jnp.bfloat16
        )
        dkv_ref[1, 0, first:last, :] = mm(probs_ref[first:last, :last], g_ref[0, :last, :]).astype(jnp.bfloat16)


def own_kernel(
    q_ref, k_ref, v_ref, g_ref, gain_ref, low_ref, stats_ref, dqh_ref,
    gq_ref, dk_ref, dv_ref, head_ref, probs_ref, grads_ref, *, factor, score_scale,
):
    rows = q_ref.shape[1]
    key_cols = k_ref[0].T
    head_sum = jnp.zeros((1, q_ref.shape[2]), jnp.float32)
    for start in range(0, rows, GROUP):
        width = min(GROUP, rows - start)
        stop = start + width
        scaled = scaled_rows(q_ref, gain_ref, start, width)
        logits = own_logits(k_ref, scaled, low_ref, start, width, factor)
        weights = jnp.exp2(logits - stats_ref[0, M_ROW : M_ROW + 1, start:stop])
        prob_grad = mm_t(v_ref[0, :stop, :], g_ref[0, start:stop, :])
        probs = (weights * stats_ref[0, L_ROW : L_ROW + 1, start:stop]).astype(jnp.bfloat16)
        delta = stats_ref[0, D_ROW : D_ROW + 1, start:stop]
        grads = (probs.astype(jnp.float32) * (prob_grad - delta)).astype(jnp.bfloat16)
        probs_ref[:stop, start:stop] = probs
        grads_ref[:stop, start:stop] = grads
        dq = mm(key_cols[:, :stop], grads).T
        halo = min(stop, PREV) - start
        if halo < width:
            zeros = jnp.zeros((width - max(halo, 0), dq.shape[1]), jnp.float32)
            extra = jnp.concatenate([dqh_ref[0, start : start + halo, :], zeros], axis=0) if halo > 0 else zeros
        else:
            extra = dqh_ref[0, start:stop, :]
        dq = (dq + extra) * score_scale
        gq_ref[0, start:stop, :] = (dq * gain_ref[0]).astype(jnp.bfloat16)
        head_sum = head_sum + jnp.sum(
            dq * q_ref[0, start:stop, :].astype(jnp.float32), axis=0, keepdims=True
        )
    head_ref[0] = head_sum
    for first in range(0, rows, GROUP):
        last = min(first + GROUP, rows)
        late_scaled = scaled_rows(q_ref, gain_ref, first, rows - first)
        dk_ref[0, first:last, :] = mm(grads_ref[first:last, first:], late_scaled) * score_scale
        dv_ref[0, first:last, :] = mm(probs_ref[first:last, first:], g_ref[0, first:, :])


def whole(shape):
    return pl.BlockSpec((1,) + shape, lambda p: (p,) + (0,) * len(shape))


def ctx_sum(value, axis):
    length = lax.axis_size(axis)
    if length > 4:
        return lax.psum(value, axis)
    total = value
    for by in range(1, length):
        total = total + shift(value, axis, by)
    return total


def on_device(queries, keys, values, grad_out, gain, doc_start, win_start):
    pair_count, rows, width = queries.shape
    score_scale = 1.0 / math.sqrt(width)
    factor = score_scale * LOG2E
    first_row = lax.axis_index("ctx") * rows
    first_pair = lax.axis_index("dp") * pair_count
    head_first = first_pair % HEADS
    seq_index = first_pair // HEADS
    aligned = lax.axis_size("dp") * pair_count == HEADS and gain.shape[0] == pair_count * width

    tail = jnp.stack([keys[:, rows - PREV :], values[:, rows - PREV :]])
    halo = shift(tail, "ctx", 1)

    if aligned:
        gain_rows = gain.reshape(pair_count, 1, width)
    else:
        full_gain = lax.all_gather(gain, "dp", axis=0, tiled=True)
        gain_rows = lax.dynamic_slice_in_dim(
            full_gain.reshape(HEADS, width), head_first, pair_count, 0
        ).reshape(pair_count, 1, width)
    lower = jnp.maximum(
        lax.dynamic_slice(doc_start, (seq_index, first_row), (1, rows)),
        lax.dynamic_slice(win_start, (seq_index, first_row), (1, rows)),
    )
    block_floor = (jnp.arange(rows, dtype=jnp.int32) // BLK - (WBLK - 1)) * BLK
    lower = jnp.maximum(lower - first_row, block_floor[None, :])

    row_spec = whole((rows, width))
    gain_spec = whole((1, width))
    stat_spec = whole((8, rows))
    prev_spec = whole((PREV, width))
    low_spec = pl.BlockSpec((1, rows), lambda p: (0, 0))
    kv_spec = pl.BlockSpec((2, 1, PREV, width), lambda p: (0, p, 0, 0))
    params = pltpu.CompilerParams(vmem_limit_bytes=48 * 1024 * 1024)
    stat_shape = jax.ShapeDtypeStruct((pair_count, 8, rows), jnp.float32)

    part = pl.pallas_call(
        functools.partial(stats_kernel, factor=factor),
        grid=(pair_count,),
        in_specs=[row_spec] * 4 + [gain_spec, low_spec],
        out_specs=stat_spec,
        out_shape=stat_shape,
        compiler_params=params,
        cost_estimate=pl.CostEstimate(flops=4 * rows * rows * width, bytes_accessed=8 * rows * width, transcendentals=rows * rows),
    )(queries, keys, values, grad_out, gain_rows, lower)

    stats, dq_halo, dkv_halo = pl.pallas_call(
        functools.partial(halo_kernel, factor=factor, score_scale=score_scale),
        grid=(pair_count,),
        in_specs=[row_spec] * 2 + [gain_spec, low_spec, stat_spec, kv_spec],
        out_specs=(stat_spec, prev_spec, kv_spec),
        out_shape=(
            stat_shape,
            jax.ShapeDtypeStruct((pair_count, PREV, width), jnp.float32),
            jax.ShapeDtypeStruct((2, pair_count, PREV, width), jnp.bfloat16),
        ),
        scratch_shapes=[pltpu.VMEM((PREV, PREV), jnp.bfloat16)] * 2,
        compiler_params=params,
        cost_estimate=pl.CostEstimate(flops=6 * rows * rows * width, bytes_accessed=8 * rows * width, transcendentals=rows * rows),
    )(queries, grad_out, gain_rows, lower, part, halo)

    returned = shift(dkv_halo, "ctx", -1)

    grad_queries, dk_own, dv_own, head_terms = pl.pallas_call(
        functools.partial(own_kernel, factor=factor, score_scale=score_scale),
        grid=(pair_count,),
        in_specs=[row_spec] * 4 + [gain_spec, low_spec, stat_spec, prev_spec],
        out_specs=(row_spec, row_spec, row_spec, gain_spec),
        out_shape=(
            jax.ShapeDtypeStruct((pair_count, rows, width), jnp.bfloat16),
            jax.ShapeDtypeStruct((pair_count, rows, width), jnp.float32),
            jax.ShapeDtypeStruct((pair_count, rows, width), jnp.float32),
            jax.ShapeDtypeStruct((pair_count, 1, width), jnp.float32),
        ),
        scratch_shapes=[pltpu.VMEM((rows, rows), jnp.bfloat16)] * 2,
        compiler_params=params,
        cost_estimate=pl.CostEstimate(flops=10 * rows * rows * width, bytes_accessed=16 * rows * width, transcendentals=rows * rows),
    )(queries, keys, values, grad_out, gain_rows, lower, stats, dq_halo)

    if aligned:
        grad_gain = ctx_sum(head_terms, "ctx").reshape(pair_count * width)
    else:
        gain_table = lax.dynamic_update_slice_in_dim(
            jnp.zeros((HEADS, width), jnp.float32), head_terms.reshape(pair_count, width), head_first, 0
        ).reshape(HEADS * width)
        everything = lax.psum(gain_table, ("ctx", "dp"))
        share = gain.shape[0]
        grad_gain = lax.dynamic_slice_in_dim(everything, lax.axis_index("dp") * share, share, 0)

    def joined(own, back):
        return own.at[:, rows - PREV :].add(back.astype(jnp.float32)).astype(jnp.bfloat16)

    return (grad_queries, joined(dk_own, returned[0]), joined(dv_own, returned[1]), grad_gain)


def solution(mesh):
    rows = P("dp", "ctx", None)
    return jax.shard_map(
        on_device,
        mesh=mesh,
        in_specs=(rows, rows, rows, rows, P("dp"), P(), P()),
        out_specs=(rows, rows, rows, P("dp")),
        check_vma=False,
    )
```

time: 117 us -> 34 us (0.29)
  blocking collectives: 56.4 us -> 0 us
  matrix products: 16.2 us -> 0 us
  other arithmetic: 17.9 us -> 2.86 us
  waiting for transfers between devices: 0.01 us -> 14.2 us
  local copies, waits for them, and re-layouts: 12.8 us -> 1.76 us
  Pallas kernels: 0 us -> 6.89 us
  starting transfers between devices: 10.8 us -> 7.32 us
  loops' own time: 1.26 us -> 0 us
    psum x1 -> x0, blocking collectives: 44.3 us -> none  [on_device(): everything = lax.psum(gain_table, ('ctx', 'dp'))]
    dot_general x80 -> x0, matrix products: 16.2 us -> none  [the longest x32 6.77 us: block_scores(): jnp.einsum('bnqd,bnkd->bnqk', left_rows, right_rows, preferred_element_ty...]
    ppermute x4 -> x5, waiting for transfers between devices: 0.01 us -> 14.2 us  [shift(): return lax.ppermute(value, axis, pairs)]
    all_gather x1 -> x0, blocking collectives: 12.1 us -> none  [on_device(): full_gain = lax.all_gather(gain, 'dp', axis=0, tiled=True)]
    pallas_call x0 -> x3, Pallas kernels: none -> 6.89 us  [the longest x1 2.85 us: on_device(): pl.pallas_call(functools.partial(own_kernel, factor=factor, score_scale=s...]
    sub x2 -> x0, other arithmetic: 5.76 us -> none  [band_terms(): prob_grad - row_delta]
    while x88 -> x0, local copies, waits for them, and re-layouts: 4.93 us -> none
    div x2 -> x0, other arithmetic: 4.93 us -> none  [band_terms(): weights / jnp.sum(weights, axis=-1, keepdims=True)]
  transfers between devices with their start and end apart: 4 -> 5, of which waited for: 0 -> 3; matrix products, arithmetic and copies ran while one was open for 6% -> 4% of each run, Pallas kernels for 0% -> 12%
where the time goes in v1:
time: 34 us; the launch traced here: 33.8 us
  waiting for transfers between devices  14.2 us (42%)
  starting transfers between devices  7.32 us (22%)
  Pallas kernels  6.89 us (20%)
  other arithmetic  2.86 us (8%)
  local copies, waits for them, and re-layouts  1.76 us (5%)
  between operations  0.73 us (2%)
    ppermute x5, waiting for transfers between devices, shift(): return lax.ppermute(value, axis, pairs)  14.2 us
    ppermute x5, starting transfers between devices, shift(): return lax.ppermute(value, axis, pairs)  7.32 us
    pallas_call x1, Pallas kernels, on_device(): pl.pallas_call(functools.partial(own_kernel, factor=factor, score_scale=s...  2.85 us
    pallas_call x1, Pallas kernels, on_device(): pl.pallas_call(functools.partial(halo_kernel, factor=factor, score_scale=...  2.79 us
    convert_element_type x2, other arithmetic, joined(): own.at[:, rows - PREV:].add(back.astype(jnp.float32)).astype(jnp.bfloat16)  1.46 us
    pallas_call x1, Pallas kernels, on_device(): pl.pallas_call(functools.partial(stats_kernel, factor=factor), grid=(pair...  1.25 us
    another operation x1, local copies, waits for them, and re-layouts, on_device(): tail = jnp.stack([keys[:, rows - PREV:], values[:, rows - PREV:]])  1.13 us
    max x1, other arithmetic, on_device(): lower = jnp.maximum(lower - first_row, block_floor[None, :])  0.72 us
  transfers between devices with their start and end apart: 5, of which 3 were waited for; matrix products, arithmetic and copies ran while one was open for 4% of the time, Pallas kernels for 12%

profile of v1, /device:TPU:0, one launch (start us, length us, event | category | flops | bytes accessed | tf_op | source)
XLA Modules:
  0.0 33.8 jit_solution(7314141048931086591)
XLA Ops:
  0.6 0.0 copy-start.3
  0.6 1.1 %slice_bitcast_fusion.2 = (bf16[1,1,896,128]{3,2,1,0:T(8,128)(2,1)S(1)}, bf16[1,1,896,128]{3,2,1,0:T(8,128)(2,1)S(1)}) fusion(bf16[1,1024,128]{2,1,0:T(8,128)(2,1)} %v_ref.3, bf16[1,1024,128]{2,1,0:T(8,128)(2,1)} %k_ref.3), kind=kLoop, calls=%fused_computation.7 | loop fusion | bytes 917504 | tf_op jit(solution)/shard_map/stack | solution.py:174
  1.8 0.0 copy-start
  1.8 0.0 copy-start.1
  1.8 0.0 copy-start.2
  1.9 3.0 %collective-permute-start = (bf16[2,1,896,128]{3,2,1,0:T(8,128)(2,1)S(1)}, bf16[2,1,896,128]{3,2,1,0:T(8,128)(2,1)S(1)}, u32[]{:S(2)}, u32[]{:S(2)}) collective-permute-start(bf16[2,1,896,128]{3,2,1,0:T(8,128)(2,1)S(1)} %pad_maximum_fusion), channel_id=1, source_target_pairs={{0,8},{8,16},{16,24},{24,0},{1,9},{9,17},{17,25},{25,1},{2,10},{10... | collective-permute-start | bytes 1376264 | tf_op jit(solution)/shard_map/ppermute | solution.py:24
  4.8 0.7 %fusion.4.low_ref = s32[1,1024]{1,0:T(1,128)S(1)} fusion(s32[1,4096]{1,0:T(1,128)} %param.17, s32[]{:T(128)S(6)} %select_n.21, s32[1,4096]{1,0:T(1,128)} %param.16, s32[]{:T(128)S(6)} %mul.14), kind=kLoop, calls=%fused_computation.15 | loop fusion | flops 13312 | bytes 12296 | tf_op jit(solution)/shard_map/max | solution.py:189
  5.6 0.0 copy-start.4
  5.6 0.0 copy-done.3
  5.6 0.0 copy-done
  5.6 0.0 copy-done.1
  5.6 0.0 copy-done.2
  5.6 0.6 %copy-done.4 = f32[128]{0:T(128)S(1)} copy-done((f32[128]{0:T(128)S(1)}, f32[128]{0:T(128)}, u32[]{:S(2)}) %copy-start.4) | copy-done | bytes 536
  6.2 1.2 %shard_map.102.part_ref = f32[1,8,1024]{2,1,0:T(8,128)S(1)} custom-call(bf16[1,1024,128]{2,1,0:T(8,128)(2,1)S(1)} %copy-done.2, bf16[1,1024,128]{2,1,0:T(8,128)(2,1)S(1)} %copy-done, bf16[1,1024,128]{2,1,0:T(8,128)(2,1)S(1)} %copy-done.1, bf16[1,1024,128]{2,1,0:T(8,128)(2,1)S(1)} %copy-done.3, f32[1,1,128]{2,1,0:T(1,128)S(1)} %bitcast.17, ...), custom_call_target="tpu_custom_call" | custom-call | flops 536870912 | bytes 1048576 | tf_op jit(solution)/shard_map/pallas_call | solution.py:200
  7.5 8.8 %collective-permute-done.kv_ref = bf16[2,1,896,128]{3,2,1,0:T(8,128)(2,1)S(1)} collective-permute-done((bf16[2,1,896,128]{3,2,1,0:T(8,128)(2,1)S(1)}, bf16[2,1,896,128]{3,2,1,0:T(8,128)(2,1)S(1)}, u32[]{:S(2)}, u32[]{:S(2)}) %collective-permute-start) | collective-permute-done | bytes 458784 | tf_op jit(solution)/shard_map/ppermute | solution.py:24
  16.3 2.8 %shard_map.103 = (f32[1,8,1024]{2,1,0:T(8,128)S(1)}, f32[1,896,128]{2,1,0:T(8,128)S(1)}, bf16[2,1,896,128]{3,2,1,0:T(8,128)(2,1)S(1)}) custom-call(bf16[1,1024,128]{2,1,0:T(8,128)(2,1)S(1)} %copy-done.2, bf16[1,1024,128]{2,1,0:T(8,128)(2,1)S(1)} %copy-done.3, f32[1,1,128]{2,1,0:T(1,128)S(1)} %bitcast.18, s32[1,1024]{1,0:T(1,128)S(1)} %fusion.4.low_ref, ...), custom_call_target="tpu_custom_call" | custom-call | flops 805306368 | bytes 1048576 | tf_op jit(solution)/shard_map/pallas_call | solution.py:210
  19.1 1.8 %collective-permute-start.1 = (bf16[2,1,896,128]{3,2,1,0:T(8,128)(2,1)S(1)}, bf16[2,1,896,128]{3,2,1,0:T(8,128)(2,1)S(1)}, u32[]{:S(2)}, u32[]{:S(2)}) collective-permute-start(bf16[2,1,896,128]{3,2,1,0:T(8,128)(2,1)S(1)} %get-tuple-element.39), channel_id=1, source_target_pairs={{0,24},{8,0},{16,8},{24,16},{1,25},{9,1},{17,9},{25,17},{2,26},{10... | collective-permute-start | bytes 1376264 | tf_op jit(solution)/shard_map/ppermute | solution.py:24
  20.9 2.9 %shard_map.104 = (bf16[1,1024,128]{2,1,0:T(8,128)(2,1)}, f32[1,1024,128]{2,1,0:T(8,128)S(1)}, f32[1,1024,128]{2,1,0:T(8,128)S(1)}, f32[1,1,128]{2,1,0:T(1,128)S(1)}) custom-call(bf16[1,1024,128]{2,1,0:T(8,128)(2,1)S(1)} %copy-done.2, bf16[1,1024,128]{2,1,0:T(8,128)(2,1)S(1)} %copy-done, bf16[1,1024,128]{2,1,0:T(8,128)(2,1)S(1)} %copy-done.1, ...), custom_call_target="tpu_custom_call" | custom-call | flops 1342177280 | bytes 2097152 | tf_op jit(solution)/shard_map/pallas_call | solution.py:227
  23.8 1.4 %collective-permute-start.4 = (f32[1,1,128]{2,1,0:T(1,128)S(1)}, f32[1,1,128]{2,1,0:T(1,128)S(1)}, u32[]{:S(2)}, u32[]{:S(2)}) collective-permute-start(f32[1,1,128]{2,1,0:T(1,128)S(1)} %get-tuple-element.41), channel_id=1, source_target_pairs={{0,24},{8,0},{16,8},{24,16},{1,25},{9,1},{17,9},{25,17},{2,26},{10... | collective-permute-start | bytes 1544 | tf_op jit(solution)/shard_map/ppermute | solution.py:24
  25.2 0.3 collective-permute-start.3
  25.5 0.8 %collective-permute-start.2 = (f32[1,1,128]{2,1,0:T(1,128)S(1)}, f32[1,1,128]{2,1,0:T(1,128)S(1)}, u32[]{:S(2)}, u32[]{:S(2)}) collective-permute-start(f32[1,1,128]{2,1,0:T(1,128)S(1)} %get-tuple-element.41), channel_id=1, source_target_pairs={{0,8},{8,16},{16,24},{24,0},{1,9},{9,17},{17,25},{25,1},{2,10},{10... | collective-permute-start | bytes 1544 | tf_op jit(solution)/shard_map/ppermute | solution.py:24
  26.3 4.6 %collective-permute-done.4 = f32[1,1,128]{2,1,0:T(1,128)S(1)} collective-permute-done((f32[1,1,128]{2,1,0:T(1,128)S(1)}, f32[1,1,128]{2,1,0:T(1,128)S(1)}, u32[]{:S(2)}, u32[]{:S(2)}) %collective-permute-start.4) | collective-permute-done | bytes 544 | tf_op jit(solution)/shard_map/ppermute | solution.py:24
  30.9 0.0 collective-permute-done.3
  30.9 0.7 %collective-permute-done.2 = f32[1,1,128]{2,1,0:T(1,128)S(1)} collective-permute-done((f32[1,1,128]{2,1,0:T(1,128)S(1)}, f32[1,1,128]{2,1,0:T(1,128)S(1)}, u32[]{:S(2)}, u32[]{:S(2)}) %collective-permute-start.2) | collective-permute-done | bytes 544 | tf_op jit(solution)/shard_map/ppermute | solution.py:24
  31.7 0.5 %add_bitcast_fusion = f32[128]{0:T(128)} fusion(f32[1,1,128]{2,1,0:T(1,128)S(1)} %collective-permute-done.4, f32[1,1,128]{2,1,0:T(1,128)S(1)} %collective-permute-done.3, f32[1,1,128]{2,1,0:T(1,128)S(1)} %get-tuple-element.41, f32[1,1,128]{2,1,0:T(1,128)S(1)} %collective-permute-done.2), kind=kLoop, calls=%fused_computation.16 | loop fusion | flops 384 | bytes 2560 | tf_op jit(solution)/shard_map/reshape | solution.py:244
  32.2 0.0 collective-permute-done.1
  32.2 0.1 fusion
  32.3 0.7 %convert_element_type.39 = bf16[1,1024,128]{2,1,0:T(8,128)(2,1)} convert(f32[1,1024,128]{2,1,0:T(8,128)S(1)} %get-tuple-element.42) | non-fusion elementwise | flops 131072 | bytes 786432 | tf_op jit(solution)/shard_map/convert_element_type | solution.py:254
  33.1 0.7 %convert_element_type.36 = bf16[1,1024,128]{2,1,0:T(8,128)(2,1)} convert(f32[1,1024,128]{2,1,0:T(8,128)S(1)} %get-tuple-element.43) | non-fusion elementwise | flops 131072 | bytes 786432 | tf_op jit(solution)/shard_map/convert_element_type | solution.py:254
  (1 shorter events, 0.0 us)
Async XLA Ops:
  0.6 5.0 %copy-start.3 = (bf16[1,1024,128]{2,1,0:T(8,128)(2,1)S(1)}, bf16[1,1024,128]{2,1,0:T(8,128)(2,1)}, u32[]{:S(2)}) copy-start(bf16[1,1024,128]{2,1,0:T(8,128)(2,1)} %g_ref.5) | copy-start | bytes 786436
  1.8 3.8 %copy-start = (bf16[1,1024,128]{2,1,0:T(8,128)(2,1)S(1)}, bf16[1,1024,128]{2,1,0:T(8,128)(2,1)}, u32[]{:S(2)}) copy-start(bf16[1,1024,128]{2,1,0:T(8,128)(2,1)} %k_ref.3) | copy-start | bytes 786436
  1.8 3.8 %copy-start.1 = (bf16[1,1024,128]{2,1,0:T(8,128)(2,1)S(1)}, bf16[1,1024,128]{2,1,0:T(8,128)(2,1)}, u32[]{:S(2)}) copy-start(bf16[1,1024,128]{2,1,0:T(8,128)(2,1)} %v_ref.3) | copy-start | bytes 786436
  1.8 3.8 %copy-start.2 = (bf16[1,1024,128]{2,1,0:T(8,128)(2,1)S(1)}, bf16[1,1024,128]{2,1,0:T(8,128)(2,1)}, u32[]{:S(2)}) copy-start(bf16[1,1024,128]{2,1,0:T(8,128)(2,1)} %q_ref.5) | copy-start | bytes 786436
  1.9 14.5 %collective-permute-start = (bf16[2,1,896,128]{3,2,1,0:T(8,128)(2,1)S(1)}, bf16[2,1,896,128]{3,2,1,0:T(8,128)(2,1)S(1)}, u32[]{:S(2)}, u32[]{:S(2)}) collective-permute-start(bf16[2,1,896,128]{3,2,1,0:T(8,128)(2,1)S(1)} %pad_maximum_fusion), channel_id=1, source_target_pairs={{0,8},{8,16},{16,24},{24,0},{1,9},{9,17},{17,25},{25,1},{2,10},{10... | collective-permute-start | bytes 1376264 | tf_op jit(solution)/shard_map/ppermute | solution.py:24
  5.6 0.7 %copy-start.4 = (f32[128]{0:T(128)S(1)}, f32[128]{0:T(128)}, u32[]{:S(2)}) copy-start(f32[128]{0:T(128)} %param.15) | copy-start | bytes 1540
  19.1 13.1 %collective-permute-start.1 = (bf16[2,1,896,128]{3,2,1,0:T(8,128)(2,1)S(1)}, bf16[2,1,896,128]{3,2,1,0:T(8,128)(2,1)S(1)}, u32[]{:S(2)}, u32[]{:S(2)}) collective-permute-start(bf16[2,1,896,128]{3,2,1,0:T(8,128)(2,1)S(1)} %get-tuple-element.39), channel_id=1, source_target_pairs={{0,24},{8,0},{16,8},{24,16},{1,25},{9,1},{17,9},{25,17},{2,26},{10... | collective-permute-start | bytes 1376264 | tf_op jit(solution)/shard_map/ppermute | solution.py:24
  23.8 7.2 %collective-permute-start.4 = (f32[1,1,128]{2,1,0:T(1,128)S(1)}, f32[1,1,128]{2,1,0:T(1,128)S(1)}, u32[]{:S(2)}, u32[]{:S(2)}) collective-permute-start(f32[1,1,128]{2,1,0:T(1,128)S(1)} %get-tuple-element.41), channel_id=1, source_target_pairs={{0,24},{8,0},{16,8},{24,16},{1,25},{9,1},{17,9},{25,17},{2,26},{10... | collective-permute-start | bytes 1544 | tf_op jit(solution)/shard_map/ppermute | solution.py:24
  25.2 5.7 %collective-permute-start.3 = (f32[1,1,128]{2,1,0:T(1,128)S(1)}, f32[1,1,128]{2,1,0:T(1,128)S(1)}, u32[]{:S(2)}, u32[]{:S(2)}) collective-permute-start(f32[1,1,128]{2,1,0:T(1,128)S(1)} %get-tuple-element.41), channel_id=1, source_target_pairs={{0,16},{8,24},{16,0},{24,8},{1,17},{9,25},{17,1},{25,9},{2,18},{10... | collective-permute-start | bytes 1544 | tf_op jit(solution)/shard_map/ppermute | solution.py:24
  25.5 6.2 %collective-permute-start.2 = (f32[1,1,128]{2,1,0:T(1,128)S(1)}, f32[1,1,128]{2,1,0:T(1,128)S(1)}, u32[]{:S(2)}, u32[]{:S(2)}) collective-permute-start(f32[1,1,128]{2,1,0:T(1,128)S(1)} %get-tuple-element.41), channel_id=1, source_target_pairs={{0,8},{8,16},{16,24},{24,0},{1,9},{9,17},{17,25},{25,1},{2,10},{10... | collective-permute-start | bytes 1544 | tf_op jit(solution)/shard_map/ppermute | solution.py:24

commit v2 on v1

v2 whole, which is shorter than its diff:
```python
import functools
import math

import jax
import jax.numpy as jnp
from jax import lax
from jax.experimental import pallas as pl
from jax.experimental.pallas import tpu as pltpu
from jax.sharding import PartitionSpec as P

HEADS = 8
BLK = 128
WBLK = 8
PREV = (WBLK - 1) * BLK
GROUP = 2 * BLK
LOG2E = 1.4426950408889634
NEG = -1e30
M_ROW, L_ROW, D_ROW = 0, 1, 2
LIGHT, HEAVY = 1, 10**10


def shift(value, axis, by):
    length = lax.axis_size(axis)
    pairs = [(i, (i + by) % length) for i in range(length)]
    return lax.ppermute(value, axis, pairs)


def mm(left, right):
    return lax.dot_general(left, right, (((1,), (0,)), ((), ())), preferred_element_type=jnp.float32)


def mm_t(left, right):
    return lax.dot_general(left, right, (((1,), (1,)), ((), ())), preferred_element_type=jnp.float32)


def groups(rows):
    return [(start, min(start + GROUP, rows)) for start in range(0, rows, GROUP)]


def halo_chunks(halo, rows):
    ahead = PREV - halo
    return [
        (max(0, start - ahead), min(halo, stop - ahead), min(stop, PREV))
        for start, stop in groups(rows)
        if start < PREV and stop > ahead
    ]


def halo_from(start, halo):
    return max(0, start - (PREV - halo))


def own_stats_kernel(
    q_hbm, k_hbm, v_hbm, g_hbm, gain_ref, low_ref,
    q_ref, g_ref, scaled_ref, keyt_ref, stats_ref, weight_ref, slope_ref, k_ref, v_ref, sems, *, factor,
):
    pair = pl.program_id(0)
    copies = [
        pltpu.make_async_copy(source.at[pair], target, sems.at[i])
        for i, (source, target) in enumerate(
            ((q_hbm, q_ref.at[0]), (k_hbm, k_ref), (v_hbm, v_ref), (g_hbm, g_ref.at[0]))
        )
    ]
    for copy in copies:
        copy.start()
    for copy in copies:
        copy.wait()
    rows = q_ref.shape[1]
    keyt_ref[0] = k_ref[...].T
    scaled_ref[0] = (q_ref[0].astype(jnp.float32) * gain_ref[0]).astype(jnp.bfloat16)
    for start, stop in groups(rows):
        logits = mm_t(k_ref[:stop, :], scaled_ref[0, start:stop, :]) * factor
        key_at = lax.broadcasted_iota(jnp.int32, logits.shape, 0)
        query_at = start + lax.broadcasted_iota(jnp.int32, logits.shape, 1)
        visible = (key_at >= low_ref[:, start:stop]) & (key_at <= query_at)
        logits = jnp.where(visible, logits, NEG)
        top = jnp.max(logits, axis=0, keepdims=True)
        weights = jnp.exp2(logits - top)
        slopes = mm_t(v_ref[:stop, :], g_ref[0, start:stop, :])
        weight_ref[0, :stop, start:stop] = weights
        slope_ref[0, :stop, start:stop] = slopes
        stats_ref[0, M_ROW : M_ROW + 1, start:stop] = top
        stats_ref[0, L_ROW : L_ROW + 1, start:stop] = jnp.sum(weights, axis=0, keepdims=True)
        stats_ref[0, D_ROW : D_ROW + 1, start:stop] = jnp.sum(weights * slopes, axis=0, keepdims=True)


def probs_kernel(
    scaled_ref, g_ref, low_ref, part_ref, weight_ref, kh_ref,
    delta_ref, hprobs_ref, probs_ref, dv_ref, *, factor,
):
    rows = scaled_ref.shape[1]
    halo = kh_ref.shape[1]
    for start, stop in groups(rows):
        own_top = part_ref[0, M_ROW : M_ROW + 1, start:stop]
        total = part_ref[0, L_ROW : L_ROW + 1, start:stop]
        if start < PREV:
            first = halo_from(start, halo)
            logits = mm_t(kh_ref[0, first:, :], scaled_ref[0, start:stop, :]) * factor
            key_at = (first - halo) + lax.broadcasted_iota(jnp.int32, logits.shape, 0)
            logits = jnp.where(key_at >= low_ref[:, start:stop], logits, NEG)
            top = jnp.maximum(own_top, jnp.max(logits, axis=0, keepdims=True))
            weights = jnp.exp2(logits - top)
            shrink = jnp.exp2(own_top - top)
            total = total * shrink + jnp.sum(weights, axis=0, keepdims=True)
            inverse = 1.0 / total
            hprobs_ref[0, first:, start:stop] = (weights * inverse).astype(jnp.bfloat16)
            share = shrink * inverse
        else:
            share = 1.0 / total
        delta_ref[0, 0:1, start:stop] = part_ref[0, D_ROW : D_ROW + 1, start:stop] * share
        probs_ref[0, :stop, start:stop] = (weight_ref[0, :stop, start:stop] * share).astype(jnp.bfloat16)
    for first, last, seen in halo_chunks(halo, rows):
        dv_ref[0, first:last, :] = mm(hprobs_ref[0, first:last, :seen], g_ref[0, :seen, :]).astype(jnp.bfloat16)


def grads_kernel(
    q_ref, scaled_ref, g_ref, keyt_ref, part_ref, hprobs_ref, probs_ref, slope_ref, kh_ref, vh_ref,
    dq_ref, dk_ref, head_ref, grads_ref, hgrads_ref, *, score_scale,
):
    rows = q_ref.shape[1]
    halo = kh_ref.shape[1]
    halo_cols = kh_ref[0].T
    head_sum = jnp.zeros((1, q_ref.shape[2]), jnp.float32)
    for start, stop in groups(rows):
        delta = part_ref[0, 0:1, start:stop]
        if start < PREV:
            first = halo_from(start, halo)
            probs = hprobs_ref[0, first:, start:stop].astype(jnp.float32)
            slopes = mm_t(vh_ref[0, first:, :], g_ref[0, start:stop, :])
            delta = delta + jnp.sum(probs * slopes, axis=0, keepdims=True)
            hgrads = (probs * (slopes - delta)).astype(jnp.bfloat16)
            hgrads_ref[first:, start:stop] = hgrads
        probs = probs_ref[0, :stop, start:stop].astype(jnp.float32)
        grads = (probs * (slope_ref[0, :stop, start:stop] - delta)).astype(jnp.bfloat16)
        grads_ref[0, :stop, start:stop] = grads
        dq = mm(keyt_ref[0, :, :stop], grads)
        if start < PREV:
            dq = dq + mm(halo_cols[:, first:], hgrads)
        dq = dq.T * score_scale
        dq_ref[0, start:stop, :] = dq
        head_sum = head_sum + jnp.sum(dq * q_ref[0, start:stop, :].astype(jnp.float32), axis=0, keepdims=True)
    head_ref[0] = head_sum
    for first, last, seen in halo_chunks(halo, rows):
        dk_ref[0, first:last, :] = (mm(hgrads_ref[first:last, :seen], scaled_ref[0, :seen, :]) * score_scale).astype(
            jnp.bfloat16
        )


def own_keys_kernel(
    g_ref, scaled_ref, probs_ref, grads_ref, dq_ref, gain_ref, back_ref, gq_ref, dv_ref, dk_ref, *, score_scale
):
    rows = g_ref.shape[1]
    gq_ref[0] = (dq_ref[0] * gain_ref[0]).astype(jnp.bfloat16)
    lead = rows - back_ref.shape[1]
    for first, last in groups(rows):
        own = mm(probs_ref[0, first:last, first:], g_ref[0, first:, :])
        cut = min(max(lead - first, 0), last - first)
        if cut:
            dv_ref[0, first : first + cut, :] = own[:cut].astype(jnp.bfloat16)
        if cut < last - first:
            back = back_ref[0, first + cut - lead : last - lead, :].astype(jnp.float32)
            dv_ref[0, first + cut : last, :] = (own[cut:] + back).astype(jnp.bfloat16)
        dk_ref[0, first:last, :] = mm(grads_ref[0, first:last, first:], scaled_ref[0, first:, :]) * score_scale


def finish_kernel(own_ref, back_ref, *refs):
    terms, (dk_ref, gain_ref) = refs[:-2], refs[-2:]
    lead = own_ref.shape[1] - back_ref.shape[1]
    if lead:
        dk_ref[0, :lead, :] = own_ref[0, :lead, :].astype(jnp.bfloat16)
    dk_ref[0, lead:, :] = (own_ref[0, lead:, :] + back_ref[0].astype(jnp.float32)).astype(jnp.bfloat16)
    total = terms[0][...]
    for term in terms[1:]:
        total = total + term[...]
    gain_ref[...] = total


def whole(shape):
    return pl.BlockSpec((1,) + shape, lambda p: (p,) + (0,) * len(shape))


def band(halo, queries, keys, values, grad_out, gain_rows, lower, aligned):
    pair_count, rows, width = queries.shape
    score_scale = 1.0 / math.sqrt(width)
    factor = score_scale * LOG2E
    bf16, f32 = jnp.bfloat16, jnp.float32
    key_halo = shift(keys[:, rows - halo :], "ctx", 1)
    value_halo = shift(values[:, rows - halo :], "ctx", 1)

    row_spec = whole((rows, width))
    gain_spec = whole((1, width))
    stat_spec = whole((8, rows))
    delta_spec = whole((1, rows))
    halo_spec = whole((halo, width))
    keyt_spec = whole((width, rows))
    own_sq = whole((rows, rows))
    halo_sq = whole((halo, rows))
    low_spec = pl.BlockSpec((1, rows), lambda p: (0, 0))
    hbm = pl.BlockSpec(memory_space=pltpu.HBM)

    def shaped(shape, dtype):
        return jax.ShapeDtypeStruct((pair_count,) + shape, dtype)

    def call(kernel, in_specs, outs, weight, scratch=(), **fixed):
        specs, shapes = zip(*outs)
        return pl.pallas_call(
            functools.partial(kernel, **fixed),
            grid=(pair_count,),
            in_specs=in_specs,
            out_specs=specs,
            out_shape=shapes,
            scratch_shapes=list(scratch),
            compiler_params=pltpu.CompilerParams(vmem_limit_bytes=32 * 1024 * 1024),
            cost_estimate=pl.CostEstimate(flops=weight, bytes_accessed=1, transcendentals=0),
        )

    row_out = (row_spec, shaped((rows, width), bf16))
    wide_out = (row_spec, shaped((rows, width), f32))
    halo_out = (halo_spec, shaped((halo, width), bf16))
    queries_in, grad_in, scaled, key_cols, part, own_weights, own_slopes = call(
        own_stats_kernel,
        [hbm] * 4 + [gain_spec, low_spec],
        (
            row_out,
            row_out,
            row_out,
            (keyt_spec, shaped((width, rows), bf16)),
            (stat_spec, shaped((8, rows), f32)),
            (own_sq, shaped((rows, rows), f32)),
            (own_sq, shaped((rows, rows), f32)),
        ),
        LIGHT,
        scratch=[pltpu.VMEM((rows, width), bf16)] * 2 + [pltpu.SemaphoreType.DMA((4,))],
        factor=factor,
    )(*(pltpu.with_memory_space_constraint(x, pltpu.HBM) for x in (queries, keys, values, grad_out)), gain_rows, lower)

    own_delta, halo_probs, own_probs, dv_halo = call(
        probs_kernel,
        [row_spec, row_spec, low_spec, stat_spec, own_sq, halo_spec],
        (
            (delta_spec, shaped((1, rows), f32)),
            (halo_sq, shaped((halo, rows), bf16)),
            (own_sq, shaped((rows, rows), bf16)),
            halo_out,
        ),
        LIGHT,
        factor=factor,
    )(scaled, grad_in, lower, part, own_weights, key_halo)
    dv_back = shift(dv_halo, "ctx", -1)

    dq, dk_halo, head_terms, own_grads = call(
        grads_kernel,
        [row_spec] * 3 + [keyt_spec, delta_spec, halo_sq, own_sq, own_sq, halo_spec, halo_spec],
        (
            wide_out,
            halo_out,
            (gain_spec, shaped((1, width), f32)),
            (own_sq, shaped((rows, rows), bf16)),
        ),
        HEAVY,
        scratch=[pltpu.VMEM((halo, rows), bf16)],
        score_scale=score_scale,
    )(
        queries_in, scaled, grad_in, key_cols, own_delta, halo_probs, own_probs, own_slopes,
        key_halo, value_halo,
    )
    dk_back = shift(dk_halo, "ctx", -1)
    terms = [head_terms]
    if aligned:
        length = lax.axis_size("ctx")
        if length <= 4:
            terms += [shift(head_terms, "ctx", by) for by in range(1, length)]
        else:
            terms = [lax.psum(head_terms, "ctx")]

    grad_queries, grad_values, dk_own = call(
        own_keys_kernel,
        [row_spec, row_spec, own_sq, own_sq, row_spec, gain_spec, halo_spec],
        (row_out, row_out, wide_out),
        LIGHT,
        score_scale=score_scale,
    )(grad_in, scaled, own_probs, own_grads, dq, gain_rows, dv_back)
    grad_keys, gain_sum = call(
        finish_kernel,
        [row_spec, halo_spec] + [gain_spec] * len(terms),
        (row_out, (gain_spec, shaped((1, width), f32))),
        LIGHT,
    )(dk_own, dk_back, *terms)
    return grad_queries, grad_keys, grad_values, gain_sum


def on_device(queries, keys, values, grad_out, gain, doc_start, win_start):
    pair_count, rows, width = queries.shape
    first_row = lax.axis_index("ctx") * rows
    first_pair = lax.axis_index("dp") * pair_count
    head_first = first_pair % HEADS
    seq_index = first_pair // HEADS
    aligned = lax.axis_size("dp") * pair_count == HEADS and gain.shape[0] == pair_count * width
    if aligned:
        gain_rows = gain.reshape(pair_count, 1, width)
    else:
        full_gain = lax.all_gather(gain, "dp", axis=0, tiled=True)
        gain_rows = lax.dynamic_slice_in_dim(
            full_gain.reshape(HEADS, width), head_first, pair_count, 0
        ).reshape(pair_count, 1, width)
    lower = jnp.maximum(
        lax.dynamic_slice(doc_start, (seq_index, first_row), (1, rows)),
        lax.dynamic_slice(win_start, (seq_index, first_row), (1, rows)),
    )
    block_floor = (jnp.arange(rows, dtype=jnp.int32) // BLK - (WBLK - 1)) * BLK
    lower = jnp.maximum(lower - first_row, block_floor[None, :])

    grad_queries, grad_keys, grad_values, gain_sum = band(
        PREV, queries, keys, values, grad_out, gain_rows, lower, aligned
    )
    if aligned:
        grad_gain = gain_sum.reshape(pair_count * width)
    else:
        gain_table = lax.dynamic_update_slice_in_dim(
            jnp.zeros((HEADS, width), jnp.float32), gain_sum.reshape(pair_count, width), head_first, 0
        ).reshape(HEADS * width)
        everything = lax.psum(gain_table, ("ctx", "dp"))
        share = gain.shape[0]
        grad_gain = lax.dynamic_slice_in_dim(everything, lax.axis_index("dp") * share, share, 0)
    return (grad_queries, grad_keys, grad_values, grad_gain)


def solution(mesh):
    rows = P("dp", "ctx", None)
    return jax.shard_map(
        on_device,
        mesh=mesh,
        in_specs=(rows, rows, rows, rows, P("dp"), P(), P()),
        out_specs=(rows, rows, rows, P("dp")),
        check_vma=False,
    )
```

time: 34 us -> 27.7 us (0.81)
  waiting for transfers between devices: 14.2 us -> 1.98 us
  starting transfers between devices: 7.32 us -> 12.3 us
  Pallas kernels: 6.89 us -> 9.23 us
  other arithmetic: 2.86 us -> 0.72 us
  local copies, waits for them, and re-layouts: 1.76 us -> 2.56 us
    ppermute x5 -> x7, waiting for transfers between devices: 14.2 us -> 1.98 us  [shift(): return lax.ppermute(value, axis, pairs)]
    ppermute x5 -> x7, starting transfers between devices: 7.32 us -> 12.3 us  [shift(): return lax.ppermute(value, axis, pairs)]
    pallas_call x3 -> x5, Pallas kernels: 6.89 us -> 9.23 us  [the longest x1 2.82 us: band(): call(own_stats_kernel, [hbm] * 4 + [gain_spec, low_spec], (row_out, row_o...]
    slice x0 -> x2, local copies, waits for them, and re-layouts: none -> 1.91 us  [the longest x1 0.96 us: band(): key_halo = shift(keys[:, rows - halo:], 'ctx', 1)]
    convert_element_type x2 -> x0, other arithmetic: 1.46 us -> none  [joined(): own.at[:, rows - PREV:].add(back.astype(jnp.float32)).astype(jnp.bfloat16)]
    another operation x1 -> x0, local copies, waits for them, and re-layouts: 1.13 us -> none  [on_device(): tail = jnp.stack([keys[:, rows - PREV:], values[:, rows - PREV:]])]
    reshape x1 -> x0, other arithmetic: 0.52 us -> none  [on_device(): grad_gain = ctx_sum(head_terms, 'ctx').reshape(pair_count * width)]
  transfers between devices with their start and end apart: 5 -> 7, of which waited for: 3 -> 4; matrix products, arithmetic and copies ran while one was open for 4% -> 6% of each run, Pallas kernels for 12% -> 31%
where the time goes in v2:
time: 27.7 us; the launch traced here: 27.5 us
  starting transfers between devices  12.3 us (44%)
  Pallas kernels  9.23 us (33%)
  local copies, waits for them, and re-layouts  2.56 us (9%)
  waiting for transfers between devices  1.98 us (7%)
  other arithmetic  0.72 us (3%)
  between operations  0.67 us (2%)
    ppermute x7, starting transfers between devices, shift(): return lax.ppermute(value, axis, pairs)  12.3 us
    pallas_call x1, Pallas kernels, band(): call(own_stats_kernel, [hbm] * 4 + [gain_spec, low_spec], (row_out, row_o...  2.82 us
    pallas_call x1, Pallas kernels, band(): call(grads_kernel, [row_spec] * 3 + [keyt_spec, delta_spec, halo_sq, own_...  2.18 us
    ppermute x7, waiting for transfers between devices, shift(): return lax.ppermute(value, axis, pairs)  1.98 us
    pallas_call x1, Pallas kernels, band(): call(probs_kernel, [row_spec, row_spec, low_spec, stat_spec, own_sq, halo...  1.85 us
    pallas_call x1, Pallas kernels, band(): call(own_keys_kernel, [row_spec, row_spec, own_sq, own_sq, row_spec, gain...  1.64 us
    slice x1, local copies, waits for them, and re-layouts, band(): key_halo = shift(keys[:, rows - halo:], 'ctx', 1)  0.96 us
    slice x1, local copies, waits for them, and re-layouts, band(): value_halo = shift(values[:, rows - halo:], 'ctx', 1)  0.95 us
  transfers between devices with their start and end apart: 7, of which 4 were waited for; matrix products, arithmetic and copies ran while one was open for 6% of the time, Pallas kernels for 31%

profile of v2, /device:TPU:0, one launch (start us, length us, event | category | flops | bytes accessed | tf_op | source)
XLA Modules:
  0.0 27.5 jit_solution(14304691896920730340)
XLA Ops:
  0.6 1.0 %slice.6 = bf16[1,896,128]{2,1,0:T(8,128)(2,1)S(1)} slice(bf16[1,1024,128]{2,1,0:T(8,128)(2,1)} %k_hbm.1), slice={[0:1], [128:1024], [0:128]} | slice | bytes 458752 | tf_op jit(solution)/shard_map/slice | solution.py:187
  1.6 3.0 %collective-permute-start = (bf16[1,896,128]{2,1,0:T(8,128)(2,1)S(1)}, bf16[1,896,128]{2,1,0:T(8,128)(2,1)S(1)}, u32[]{:S(2)}, u32[]{:S(2)}) collective-permute-start(bf16[1,896,128]{2,1,0:T(8,128)(2,1)S(1)} %slice.6), channel_id=1, source_target_pairs={{0,8},{8,16},{16,24},{24,0},{1,9},{9,17},{17,25},{25,1},{2,10},{10... | collective-permute-start | bytes 688136 | tf_op jit(solution)/shard_map/ppermute | solution.py:25
  4.6 1.0 %slice.7 = bf16[1,896,128]{2,1,0:T(8,128)(2,1)S(1)} slice(bf16[1,1024,128]{2,1,0:T(8,128)(2,1)} %v_hbm.1), slice={[0:1], [128:1024], [0:128]} | slice | bytes 458752 | tf_op jit(solution)/shard_map/slice | solution.py:188
  5.5 1.5 %collective-permute-start.1 = (bf16[1,896,128]{2,1,0:T(8,128)(2,1)S(1)}, bf16[1,896,128]{2,1,0:T(8,128)(2,1)S(1)}, u32[]{:S(2)}, u32[]{:S(2)}) collective-permute-start(bf16[1,896,128]{2,1,0:T(8,128)(2,1)S(1)} %slice.7), channel_id=1, source_target_pairs={{0,8},{8,16},{16,24},{24,0},{1,9},{9,17},{17,25},{25,1},{2,10},{10... | collective-permute-start | bytes 688136 | tf_op jit(solution)/shard_map/ppermute | solution.py:25
  7.1 0.7 %fusion.2.low_ref = s32[1,1024]{1,0:T(1,128)S(1)} fusion(s32[1,4096]{1,0:T(1,128)} %param.13, s32[]{:T(128)S(6)} %select_n.21, s32[1,4096]{1,0:T(1,128)} %param.12, s32[]{:T(128)S(6)} %mul.14), kind=kLoop, calls=%fused_computation.6 | loop fusion | flops 13312 | bytes 12296 | tf_op jit(solution)/shard_map/max | solution.py:311
  7.8 0.0 copy-start
  7.8 0.6 %copy-done = f32[128]{0:T(128)S(1)} copy-done((f32[128]{0:T(128)S(1)}, f32[128]{0:T(128)}, u32[]{:S(2)}) %copy-start) | copy-done | bytes 536
  8.5 2.8 %shard_map.102 = (bf16[1,1024,128]{2,1,0:T(8,128)(2,1)S(1)}, bf16[1,1024,128]{2,1,0:T(8,128)(2,1)S(1)}, bf16[1,1024,128]{2,1,0:T(8,128)(2,1)S(1)}, bf16[1,128,10...) custom-call(bf16[1,1024,128]{2,1,0:T(8,128)(2,1)} %q_hbm.1, ...), custom_call_target="tpu_custom_call" | custom-call | flops 1 | bytes 1 | tf_op jit(solution)/shard_map/pallas_call | solution.py:220
  11.3 0.7 %collective-permute-done.kh_ref = bf16[1,896,128]{2,1,0:T(8,128)(2,1)S(1)} collective-permute-done((bf16[1,896,128]{2,1,0:T(8,128)(2,1)S(1)}, bf16[1,896,128]{2,1,0:T(8,128)(2,1)S(1)}, u32[]{:S(2)}, u32[]{:S(2)}) %collective-permute-start) | collective-permute-done | bytes 229408 | tf_op jit(solution)/shard_map/ppermute | solution.py:25
  12.0 1.8 %shard_map.103 = (f32[1,1,1024]{2,1,0:T(1,128)S(1)}, bf16[1,896,1024]{2,1,0:T(8,128)(2,1)S(1)}, bf16[1,1024,1024]{2,1,0:T(8,128)(2,1)S(1)}, bf16[1,896,128]{2,1,0:T(8,128)(2,1)S(1)}) custom-call(bf16[1,1024,128]{2,1,0:T(8,128)(2,1)S(1)} %get-tuple-element.25.scaled_ref, bf16[1,1024,128]{2,1,0:T(8,128)(2,1)S(1)} %get-tuple-element.24.g_ref, ...), custom_call_target="tpu_custom_call" | custom-call | flops 1 | bytes 1 | tf_op jit(solution)/shard_map/pallas_call | solution.py:237
  13.8 2.1 %collective-permute-start.2 = (bf16[1,896,128]{2,1,0:T(8,128)(2,1)S(1)}, bf16[1,896,128]{2,1,0:T(8,128)(2,1)S(1)}, u32[]{:S(2)}, u32[]{:S(2)}) collective-permute-start(bf16[1,896,128]{2,1,0:T(8,128)(2,1)S(1)} %get-tuple-element.36), channel_id=1, source_target_pairs={{0,24},{8,0},{16,8},{24,16},{1,25},{9,1},{17,9},{25,17},{2,26},{10... | collective-permute-start | bytes 688136 | tf_op jit(solution)/shard_map/ppermute | solution.py:25
  15.9 0.4 %collective-permute-done.1.vh_ref = bf16[1,896,128]{2,1,0:T(8,128)(2,1)S(1)} collective-permute-done((bf16[1,896,128]{2,1,0:T(8,128)(2,1)S(1)}, bf16[1,896,128]{2,1,0:T(8,128)(2,1)S(1)}, u32[]{:S(2)}, u32[]{:S(2)}) %collective-permute-start.1) | collective-permute-done | bytes 229408 | tf_op jit(solution)/shard_map/ppermute | solution.py:25
  16.3 0.0 copy-start.1
  16.3 2.2 %shard_map.104 = (f32[1,1024,128]{2,1,0:T(8,128)S(1)}, bf16[1,896,128]{2,1,0:T(8,128)(2,1)S(1)}, f32[1,1,128]{2,1,0:T(1,128)S(1)}, bf16[1,1024,1024]{2,1,0:T(8,128)(2,1)S(1)}) custom-call(bf16[1,1024,128]{2,1,0:T(8,128)(2,1)S(1)} %get-tuple-element.29.q_ref, bf16[1,1024,128]{2,1,0:T(8,128)(2,1)S(1)} %get-tuple-element.25.scaled_ref, ...), custom_call_target="tpu_custom_call" | custom-call | flops 10000000000 | bytes 1 | tf_op jit(solution)/shard_map/pallas_call | solution.py:251
  18.5 1.8 %collective-permute-start.3 = (bf16[1,896,128]{2,1,0:T(8,128)(2,1)S(1)}, bf16[1,896,128]{2,1,0:T(8,128)(2,1)S(1)}, u32[]{:S(2)}, u32[]{:S(2)}) collective-permute-start(bf16[1,896,128]{2,1,0:T(8,128)(2,1)S(1)} %get-tuple-element.39), channel_id=1, source_target_pairs={{0,24},{8,0},{16,8},{24,16},{1,25},{9,1},{17,9},{25,17},{2,26},{10... | collective-permute-start | bytes 688136 | tf_op jit(solution)/shard_map/ppermute | solution.py:25
  20.3 0.3 collective-permute-start.4
  20.6 2.6 %collective-permute-start.5 = (f32[1,1,128]{2,1,0:T(1,128)S(1)}, f32[1,1,128]{2,1,0:T(1,128)S(1)}, u32[]{:S(2)}, u32[]{:S(2)}) collective-permute-start(f32[1,1,128]{2,1,0:T(1,128)S(1)} %get-tuple-element.40.refs_0_), channel_id=1, source_target_pairs={{0,16},{8,24},{16,0},{24,8},{1,17},{9,25},{17,1},{25,9},{2,18},{10... | collective-permute-start | bytes 1544 | tf_op jit(solution)/shard_map/ppermute | solution.py:25
  23.2 1.0 %collective-permute-start.6 = (f32[1,1,128]{2,1,0:T(1,128)S(1)}, f32[1,1,128]{2,1,0:T(1,128)S(1)}, u32[]{:S(2)}, u32[]{:S(2)}) collective-permute-start(f32[1,1,128]{2,1,0:T(1,128)S(1)} %get-tuple-element.40.refs_0_), channel_id=1, source_target_pairs={{0,24},{8,0},{16,8},{24,16},{1,25},{9,1},{17,9},{25,17},{2,26},{10... | collective-permute-start | bytes 1544 | tf_op jit(solution)/shard_map/ppermute | solution.py:25
  24.1 0.0 collective-permute-done.2.back_ref
  24.2 0.0 copy-done.1
  24.2 1.6 %shard_map.105 = (bf16[1,1024,128]{2,1,0:T(8,128)(2,1)}, bf16[1,1024,128]{2,1,0:T(8,128)(2,1)}, f32[1,1024,128]{2,1,0:T(8,128)S(1)}) custom-call(bf16[1,1024,128]{2,1,0:T(8,128)(2,1)S(1)} %get-tuple-element.24.g_ref, bf16[1,1024,128]{2,1,0:T(8,128)(2,1)S(1)} %get-tuple-element.25.scaled_ref, bf16[1,1024,1024]{2,1,0:T(8,128)(2,1)S(1)} %get-tuple-element.28.probs_ref, ...), custom_call_target="tpu_custom_call" | custom-call | flops 1 | bytes 1 | tf_op jit(solution)/shard_map/pallas_call | solution.py:276
  25.8 0.8 %collective-permute-done.4.refs_1_ = f32[1,1,128]{2,1,0:T(1,128)S(1)} collective-permute-done((f32[1,1,128]{2,1,0:T(1,128)S(1)}, f32[1,1,128]{2,1,0:T(1,128)S(1)}, u32[]{:S(2)}, u32[]{:S(2)}) %collective-permute-start.4) | collective-permute-done | bytes 544 | tf_op jit(solution)/shard_map/ppermute | solution.py:25
  26.6 0.0 collective-permute-done.5.refs_2_
  26.6 0.1 collective-permute-done.6.refs_3_
  26.7 0.0 collective-permute-done.3.back_ref
  26.7 0.7 %shard_map.106 = (bf16[1,1024,128]{2,1,0:T(8,128)(2,1)}, f32[1,1,128]{2,1,0:T(1,128)}) custom-call(f32[1,1024,128]{2,1,0:T(8,128)S(1)} %get-tuple-element.38.own_ref, bf16[1,896,128]{2,1,0:T(8,128)(2,1)S(1)} %collective-permute-done.3.back_ref, f32[1,1,128]{2,1,0:T(1,128)S(1)} %get-tuple-element.40.refs_0_, f32[1,1,128]{2,1,0:T(1,128)S(1)} %collective-permute-done.4.refs_1_, ...), custom_call_target="tpu_custom_call" | custom-call | flops 1 | bytes 1 | tf_op jit(solution)/shard_map/pallas_call | solution.py:283
Async XLA Ops:
  1.6 10.4 %collective-permute-start = (bf16[1,896,128]{2,1,0:T(8,128)(2,1)S(1)}, bf16[1,896,128]{2,1,0:T(8,128)(2,1)S(1)}, u32[]{:S(2)}, u32[]{:S(2)}) collective-permute-start(bf16[1,896,128]{2,1,0:T(8,128)(2,1)S(1)} %slice.6), channel_id=1, source_target_pairs={{0,8},{8,16},{16,24},{24,0},{1,9},{9,17},{17,25},{25,1},{2,10},{10... | collective-permute-start | bytes 688136 | tf_op jit(solution)/shard_map/ppermute | solution.py:25
  5.5 10.8 %collective-permute-start.1 = (bf16[1,896,128]{2,1,0:T(8,128)(2,1)S(1)}, bf16[1,896,128]{2,1,0:T(8,128)(2,1)S(1)}, u32[]{:S(2)}, u32[]{:S(2)}) collective-permute-start(bf16[1,896,128]{2,1,0:T(8,128)(2,1)S(1)} %slice.7), channel_id=1, source_target_pairs={{0,8},{8,16},{16,24},{24,0},{1,9},{9,17},{17,25},{25,1},{2,10},{10... | collective-permute-start | bytes 688136 | tf_op jit(solution)/shard_map/ppermute | solution.py:25
  7.8 0.7 %copy-start = (f32[128]{0:T(128)S(1)}, f32[128]{0:T(128)}, u32[]{:S(2)}) copy-start(f32[128]{0:T(128)} %param.11) | copy-start | bytes 1540
  13.8 10.3 %collective-permute-start.2 = (bf16[1,896,128]{2,1,0:T(8,128)(2,1)S(1)}, bf16[1,896,128]{2,1,0:T(8,128)(2,1)S(1)}, u32[]{:S(2)}, u32[]{:S(2)}) collective-permute-start(bf16[1,896,128]{2,1,0:T(8,128)(2,1)S(1)} %get-tuple-element.36), channel_id=1, source_target_pairs={{0,24},{8,0},{16,8},{24,16},{1,25},{9,1},{17,9},{25,17},{2,26},{10... | collective-permute-start | bytes 688136 | tf_op jit(solution)/shard_map/ppermute | solution.py:25
  16.3 7.9 %copy-start.1 = (f32[128]{0:T(128)S(1)}, f32[128]{0:T(128)}, u32[]{:S(2)}) copy-start(f32[128]{0:T(128)} %param.11) | copy-start | bytes 1540
  18.5 8.2 %collective-permute-start.3 = (bf16[1,896,128]{2,1,0:T(8,128)(2,1)S(1)}, bf16[1,896,128]{2,1,0:T(8,128)(2,1)S(1)}, u32[]{:S(2)}, u32[]{:S(2)}) collective-permute-start(bf16[1,896,128]{2,1,0:T(8,128)(2,1)S(1)} %get-tuple-element.39), channel_id=1, source_target_pairs={{0,24},{8,0},{16,8},{24,16},{1,25},{9,1},{17,9},{25,17},{2,26},{10... | collective-permute-start | bytes 688136 | tf_op jit(solution)/shard_map/ppermute | solution.py:25
  20.3 6.3 %collective-permute-start.4 = (f32[1,1,128]{2,1,0:T(1,128)S(1)}, f32[1,1,128]{2,1,0:T(1,128)S(1)}, u32[]{:S(2)}, u32[]{:S(2)}) collective-permute-start(f32[1,1,128]{2,1,0:T(1,128)S(1)} %get-tuple-element.40.refs_0_), channel_id=1, source_target_pairs={{0,8},{8,16},{16,24},{24,0},{1,9},{9,17},{17,25},{25,1},{2,10},{10... | collective-permute-start | bytes 1544 | tf_op jit(solution)/shard_map/ppermute | solution.py:25
  20.6 6.0 %collective-permute-start.5 = (f32[1,1,128]{2,1,0:T(1,128)S(1)}, f32[1,1,128]{2,1,0:T(1,128)S(1)}, u32[]{:S(2)}, u32[]{:S(2)}) collective-permute-start(f32[1,1,128]{2,1,0:T(1,128)S(1)} %get-tuple-element.40.refs_0_), channel_id=1, source_target_pairs={{0,16},{8,24},{16,0},{24,8},{1,17},{9,25},{17,1},{25,9},{2,18},{10... | collective-permute-start | bytes 1544 | tf_op jit(solution)/shard_map/ppermute | solution.py:25
  23.2 3.5 %collective-permute-start.6 = (f32[1,1,128]{2,1,0:T(1,128)S(1)}, f32[1,1,128]{2,1,0:T(1,128)S(1)}, u32[]{:S(2)}, u32[]{:S(2)}) collective-permute-start(f32[1,1,128]{2,1,0:T(1,128)S(1)} %get-tuple-element.40.refs_0_), channel_id=1, source_target_pairs={{0,24},{8,0},{16,8},{24,16},{1,25},{9,1},{17,9},{25,17},{2,26},{10... | collective-permute-start | bytes 1544 | tf_op jit(solution)/shard_map/ppermute | solution.py:25

commit v3 on v2

--- a/solution.py
+++ b/solution.py
@@ -17,6 +17,8 @@
 NEG = -1e30
 M_ROW, L_ROW, D_ROW = 0, 1, 2
 LIGHT, HEAVY = 1, 10**10
+FEWEST = 3
+RIDERS = 16
 
 
 def shift(value, axis, by):
@@ -50,33 +52,52 @@
     return max(0, start - (PREV - halo))
 
 
-def own_stats_kernel(
-    q_hbm, k_hbm, v_hbm, g_hbm, gain_ref, low_ref,
-    q_ref, g_ref, scaled_ref, keyt_ref, stats_ref, weight_ref, slope_ref, k_ref, v_ref, sems, *, factor,
+def load_kernel(
+    doc_hbm, win_hbm, k_hbm, v_hbm, q_hbm, g_hbm,
+    k_ref, v_ref, q_ref, g_ref, low_ref, size_ref, doc_ref, win_ref, sems,
 ):
     pair = pl.program_id(0)
-    copies = [
-        pltpu.make_async_copy(source.at[pair], target, sems.at[i])
-        for i, (source, target) in enumerate(
-            ((q_hbm, q_ref.at[0]), (k_hbm, k_ref), (v_hbm, v_ref), (g_hbm, g_ref.at[0]))
-        )
+    moves = [(doc_hbm, doc_ref), (win_hbm, win_ref)]
+    moves += [
+        (source.at[pair], target.at[0])
+        for source, target in ((k_hbm, k_ref), (v_hbm, v_ref), (q_hbm, q_ref), (g_hbm, g_ref))
     ]
+    copies = [pltpu.make_async_copy(source, target, sems.at[i]) for i, (source, target) in enumerate(moves)]
     for copy in copies:
         copy.start()
-    for copy in copies:
+    rows = q_ref.shape[1]
+    copies[0].wait()
+    copies[1].wait()
+    reach = jnp.zeros((), jnp.int32)
+    for first in range(0, doc_ref.shape[1], rows):
+        reach = jnp.maximum(
+            reach, first - jnp.min(jnp.maximum(doc_ref[:, first : first + rows], win_ref[:, first : first + rows]))
+        )
+    size_ref[0] = jnp.clip((reach + BLK - 1) // BLK, FEWEST, WBLK - 1) - FEWEST
+    first_row = pl.multiple_of(lax.axis_index("ctx") * rows, BLK)
+    seq_index = lax.axis_index("dp") * pl.num_programs(0) // HEADS
+    own = (pl.ds(seq_index, 1), pl.ds(first_row, rows))
+    low_ref[...] = jnp.maximum(doc_ref[own], win_ref[own]) - first_row
+    for copy in copies[2:]:
         copy.wait()
+
+
+def own_stats_kernel(
+    q_ref, k_ref, v_ref, g_ref, gain_ref, low_ref,
+    scaled_ref, keyt_ref, stats_ref, weight_ref, slope_ref, *, factor,
+):
     rows = q_ref.shape[1]
-    keyt_ref[0] = k_ref[...].T
+    keyt_ref[0] = k_ref[0].T
     scaled_ref[0] = (q_ref[0].astype(jnp.float32) * gain_ref[0]).astype(jnp.bfloat16)
     for start, stop in groups(rows):
-        logits = mm_t(k_ref[:stop, :], scaled_ref[0, start:stop, :]) * factor
+        logits = mm_t(k_ref[0, :stop, :], scaled_ref[0, start:stop, :]) * factor
         key_at = lax.broadcasted_iota(jnp.int32, logits.shape, 0)
         query_at = start + lax.broadcasted_iota(jnp.int32, logits.shape, 1)
         visible = (key_at >= low_ref[:, start:stop]) & (key_at <= query_at)
         logits = jnp.where(visible, logits, NEG)
         top = jnp.max(logits, axis=0, keepdims=True)
         weights = jnp.exp2(logits - top)
-        slopes = mm_t(v_ref[:stop, :], g_ref[0, start:stop, :])
+        slopes = mm_t(v_ref[0, :stop, :], g_ref[0, start:stop, :])
         weight_ref[0, :stop, start:stop] = weights
         slope_ref[0, :stop, start:stop] = slopes
         stats_ref[0, M_ROW : M_ROW + 1, start:stop] = top
@@ -97,7 +118,9 @@
             first = halo_from(start, halo)
             logits = mm_t(kh_ref[0, first:, :], scaled_ref[0, start:stop, :]) * factor
             key_at = (first - halo) + lax.broadcasted_iota(jnp.int32, logits.shape, 0)
-            logits = jnp.where(key_at >= low_ref[:, start:stop], logits, NEG)
+            query_block = start + lax.broadcasted_iota(jnp.int32, (1, stop - start), 1) & -BLK
+            lowest = jnp.maximum(low_ref[:, start:stop], query_block - PREV)
+            logits = jnp.where(key_at >= lowest, logits, NEG)
             top = jnp.maximum(own_top, jnp.max(logits, axis=0, keepdims=True))
             weights = jnp.exp2(logits - top)
             shrink = jnp.exp2(own_top - top)
@@ -140,6 +163,13 @@
         dq_ref[0, start:stop, :] = dq
         head_sum = head_sum + jnp.sum(dq * q_ref[0, start:stop, :].astype(jnp.float32), axis=0, keepdims=True)
     head_ref[0] = head_sum
+    rest = head_sum
+    riders = []
+    for _ in range(3):
+        riders.append(rest.astype(jnp.bfloat16))
+        rest = rest - riders[-1].astype(jnp.float32)
+    filler = jnp.zeros((RIDERS - 3, head_sum.shape[1]), jnp.bfloat16)
+    dk_ref[0, halo:, :] = jnp.concatenate(riders + [filler], axis=0)
     for first, last, seen in halo_chunks(halo, rows):
         dk_ref[0, first:last, :] = (mm(hgrads_ref[first:last, :seen], scaled_ref[0, :seen, :]) * score_scale).astype(
             jnp.bfloat16
@@ -163,66 +193,68 @@
         dk_ref[0, first:last, :] = mm(grads_ref[0, first:last, first:], scaled_ref[0, first:, :]) * score_scale
 
 
-def finish_kernel(own_ref, back_ref, *refs):
+def finish_kernel(own_ref, back_ref, *refs, riding):
     terms, (dk_ref, gain_ref) = refs[:-2], refs[-2:]
-    lead = own_ref.shape[1] - back_ref.shape[1]
+    halo = back_ref.shape[1] - RIDERS
+    lead = own_ref.shape[1] - halo
     if lead:
         dk_ref[0, :lead, :] = own_ref[0, :lead, :].astype(jnp.bfloat16)
-    dk_ref[0, lead:, :] = (own_ref[0, lead:, :] + back_ref[0].astype(jnp.float32)).astype(jnp.bfloat16)
-    total = terms[0][...]
+    dk_ref[0, lead:, :] = (own_ref[0, lead:, :] + back_ref[0, :halo, :].astype(jnp.float32)).astype(jnp.bfloat16)
+    total = terms[0][0]
     for term in terms[1:]:
-        total = total + term[...]
-    gain_ref[...] = total
+        total = total + term[0]
+    if riding:
+        total = total + jnp.sum(back_ref[0, halo:, :].astype(jnp.float32), axis=0, keepdims=True)
+    gain_ref[0] = total
 
 
 def whole(shape):
     return pl.BlockSpec((1,) + shape, lambda p: (p,) + (0,) * len(shape))
 
 
-def band(halo, queries, keys, values, grad_out, gain_rows, lower, aligned):
-    pair_count, rows, width = queries.shape
+def call(kernel, pair_count, in_specs, outs, weight, scratch=(), **fixed):
+    specs, shapes = zip(*outs)
+    return pl.pallas_call(
+        functools.partial(kernel, **fixed),
+        grid=(pair_count,),
+        in_specs=in_specs,
+        out_specs=specs,
+        out_shape=shapes,
+        scratch_shapes=list(scratch),
+        compiler_params=pltpu.CompilerParams(vmem_limit_bytes=32 * 1024 * 1024),
+        cost_estimate=pl.CostEstimate(flops=weight, bytes_accessed=1, transcendentals=0),
+    )
+
+
+def band(halo, aligned, keys_in, values_in, queries_in, grad_in, lower, gain_rows):
+    pair_count, rows, width = queries_in.shape
     score_scale = 1.0 / math.sqrt(width)
     factor = score_scale * LOG2E
     bf16, f32 = jnp.bfloat16, jnp.float32
-    key_halo = shift(keys[:, rows - halo :], "ctx", 1)
-    value_halo = shift(values[:, rows - halo :], "ctx", 1)
+    key_halo = shift(keys_in[:, rows - halo :], "ctx", 1)
+    value_halo = shift(values_in[:, rows - halo :], "ctx", 1)
 
     row_spec = whole((rows, width))
     gain_spec = whole((1, width))
     stat_spec = whole((8, rows))
     delta_spec = whole((1, rows))
     halo_spec = whole((halo, width))
+    ridden_spec = whole((halo + RIDERS, width))
     keyt_spec = whole((width, rows))
     own_sq = whole((rows, rows))
     halo_sq = whole((halo, rows))
     low_spec = pl.BlockSpec((1, rows), lambda p: (0, 0))
-    hbm = pl.BlockSpec(memory_space=pltpu.HBM)
 
     def shaped(shape, dtype):
         return jax.ShapeDtypeStruct((pair_count,) + shape, dtype)
 
-    def call(kernel, in_specs, outs, weight, scratch=(), **fixed):
-        specs, shapes = zip(*outs)
-        return pl.pallas_call(
-            functools.partial(kernel, **fixed),
-            grid=(pair_count,),
-            in_specs=in_specs,
-            out_specs=specs,
-            out_shape=shapes,
-            scratch_shapes=list(scratch),
-            compiler_params=pltpu.CompilerParams(vmem_limit_bytes=32 * 1024 * 1024),
-            cost_estimate=pl.CostEstimate(flops=weight, bytes_accessed=1, transcendentals=0),
-        )
-
     row_out = (row_spec, shaped((rows, width), bf16))
     wide_out = (row_spec, shaped((rows, width), f32))
-    halo_out = (halo_spec, shaped((halo, width), bf16))
-    queries_in, grad_in, scaled, key_cols, part, own_weights, own_slopes = call(
+    scaled, key_cols, part, own_weights, own_slopes = call(
         own_stats_kernel,
-        [hbm] * 4 + [gain_spec, low_spec],
+        pair_count,
+        [row_spec] * 4 + [gain_spec, low_spec],
         (
-            row_out,
-            row_out,
             row_out,
             (keyt_spec, shaped((width, rows), bf16)),
             (stat_spec, shaped((8, rows), f32)),
@@ -230,18 +262,18 @@
             (own_sq, shaped((rows, rows), f32)),
         ),
         LIGHT,
-        scratch=[pltpu.VMEM((rows, width), bf16)] * 2 + [pltpu.SemaphoreType.DMA((4,))],
         factor=factor,
-    )(*(pltpu.with_memory_space_constraint(x, pltpu.HBM) for x in (queries, keys, values, grad_out)), gain_rows, lower)
+    )(queries_in, keys_in, values_in, grad_in, gain_rows, lower)
 
     own_delta, halo_probs, own_probs, dv_halo = call(
         probs_kernel,
+        pair_count,
         [row_spec, row_spec, low_spec, stat_spec, own_sq, halo_spec],
         (
             (delta_spec, shaped((1, rows), f32)),
             (halo_sq, shaped((halo, rows), bf16)),
             (own_sq, shaped((rows, rows), bf16)),
-            halo_out,
+            (halo_spec, shaped((halo, width), bf16)),
         ),
         LIGHT,
         factor=factor,
@@ -250,10 +282,11 @@
 
     dq, dk_halo, head_terms, own_grads = call(
         grads_kernel,
+        pair_count,
         [row_spec] * 3 + [keyt_spec, delta_spec, halo_sq, own_sq, own_sq, halo_spec, halo_spec],
         (
             wide_out,
-            halo_out,
+            (ridden_spec, shaped((halo + RIDERS, width), bf16)),
             (gain_spec, shaped((1, width), f32)),
             (own_sq, shaped((rows, rows), bf16)),
         ),
@@ -265,36 +298,36 @@
         key_halo, value_halo,
     )
     dk_back = shift(dk_halo, "ctx", -1)
+    length = lax.axis_size("ctx")
+    riding = aligned and 1 < length <= 4
     terms = [head_terms]
-    if aligned:
-        length = lax.axis_size("ctx")
-        if length <= 4:
-            terms += [shift(head_terms, "ctx", by) for by in range(1, length)]
-        else:
-            terms = [lax.psum(head_terms, "ctx")]
+    if riding:
+        terms += [shift(head_terms, "ctx", by) for by in range(1, length - 1)]
+    elif aligned:
+        terms = [lax.psum(head_terms, "ctx")]
 
     grad_queries, grad_values, dk_own = call(
         own_keys_kernel,
+        pair_count,
         [row_spec, row_spec, own_sq, own_sq, row_spec, gain_spec, halo_spec],
         (row_out, row_out, wide_out),
-        LIGHT,
+        10**9,
         score_scale=score_scale,
     )(grad_in, scaled, own_probs, own_grads, dq, gain_rows, dv_back)
     grad_keys, gain_sum = call(
         finish_kernel,
-        [row_spec, halo_spec] + [gain_spec] * len(terms),
+        pair_count,
+        [row_spec, ridden_spec] + [gain_spec] * len(terms),
         (row_out, (gain_spec, shaped((1, width), f32))),
         LIGHT,
+        riding=riding,
     )(dk_own, dk_back, *terms)
     return grad_queries, grad_keys, grad_values, gain_sum
 
 
 def on_device(queries, keys, values, grad_out, gain, doc_start, win_start):
     pair_count, rows, width = queries.shape
-    first_row = lax.axis_index("ctx") * rows
-    first_pair = lax.axis_index("dp") * pair_count
-    head_first = first_pair % HEADS
-    seq_index = first_pair // HEADS
+    head_first = lax.axis_index("dp") * pair_count % HEADS
     aligned = lax.axis_size("dp") * pair_count == HEADS and gain.shape[0] == pair_count * width
     if aligned:
         gain_rows = gain.reshape(pair_count, 1, width)
@@ -303,15 +336,25 @@
         gain_rows = lax.dynamic_slice_in_dim(
             full_gain.reshape(HEADS, width), head_first, pair_count, 0
         ).reshape(pair_count, 1, width)
-    lower = jnp.maximum(
-        lax.dynamic_slice(doc_start, (seq_index, first_row), (1, rows)),
-        lax.dynamic_slice(win_start, (seq_index, first_row), (1, rows)),
-    )
-    block_floor = (jnp.arange(rows, dtype=jnp.int32) // BLK - (WBLK - 1)) * BLK
-    lower = jnp.maximum(lower - first_row, block_floor[None, :])
-
-    grad_queries, grad_keys, grad_values, gain_sum = band(
-        PREV, queries, keys, values, grad_out, gain_rows, lower, aligned
+
+    hbm = pl.BlockSpec(memory_space=pltpu.HBM)
+    row_out = (whole((rows, width)), jax.ShapeDtypeStruct((pair_count, rows, width), jnp.bfloat16))
+    *loaded, size = call(
+        load_kernel,
+        pair_count,
+        [hbm] * 6,
+        [row_out] * 4
+        + [
+            (pl.BlockSpec((1, rows), lambda p: (0, 0)), jax.ShapeDtypeStruct((1, rows), jnp.int32)),
+            (pl.BlockSpec(memory_space=pltpu.SMEM), jax.ShapeDtypeStruct((1,), jnp.int32)),
+        ],
+        LIGHT,
+        scratch=[pltpu.VMEM(doc_start.shape, jnp.int32)] * 2 + [pltpu.SemaphoreType.DMA((6,))],
+    )(*(pltpu.with_memory_space_constraint(x, pltpu.HBM) for x in (doc_start, win_start, keys, values, queries, grad_out)))
+    grad_queries, grad_keys, grad_values, gain_sum = lax.switch(
+        size[0],
+        [functools.partial(band, blocks * BLK, aligned) for blocks in range(FEWEST, WBLK)],
+        *loaded, gain_rows,
     )
     if aligned:
         grad_gain = gain_sum.reshape(pair_count * width)

time: 27.7 us -> 22.3 us (0.81)
  starting transfers between devices: 12.3 us -> 9.2 us
  local copies, waits for them, and re-layouts: 2.56 us -> 0.02 us
  other arithmetic: 0.72 us -> 0 us
  between operations: 0.67 us -> 1.29 us
  waiting for transfers between devices: 1.98 us -> 2.35 us
    ppermute x7 -> x6, starting transfers between devices: 12.3 us -> 9.2 us  [shift(): return lax.ppermute(value, axis, pairs)]
    slice x2, local copies, waits for them, and re-layouts: 1.91 us -> 0.02 us  [the longest x1 0.01 us: band(): key_halo = shift(keys_in[:, rows - halo:], 'ctx', 1)]
    max x1 -> x0, other arithmetic: 0.72 us -> none  [on_device(): lower = jnp.maximum(lower - first_row, block_floor[None, :])]
    unnamed x4 -> x0, local copies, waits for them, and re-layouts: 0.65 us -> none
    ppermute x7 -> x6, waiting for transfers between devices: 1.98 us -> 2.35 us  [shift(): return lax.ppermute(value, axis, pairs)]
    pallas_call x5 -> x6, Pallas kernels: 9.23 us -> 9.14 us  [the longest x1 2.25 us: band(): call(own_stats_kernel, pair_count, [row_spec] * 4 + [gain_spec, low_spec]...]
  transfers between devices with their start and end apart: 7 -> 6, of which waited for: 4 -> 2; matrix products, arithmetic and copies ran while one was open for 6% -> 0% of each run, Pallas kernels for 31% -> 30%
where the time goes in v3:
time: 22.3 us; the launch traced here: 22.1 us
  starting transfers between devices  9.2 us (41%)
  Pallas kernels  9.14 us (41%)
  waiting for transfers between devices  2.35 us (11%)
  between operations  1.29 us (6%)
    ppermute x6, starting transfers between devices, shift(): return lax.ppermute(value, axis, pairs)  9.2 us
    ppermute x6, waiting for transfers between devices, shift(): return lax.ppermute(value, axis, pairs)  2.35 us
    pallas_call x1, Pallas kernels, band(): call(own_stats_kernel, pair_count, [row_spec] * 4 + [gain_spec, low_spec]...  2.25 us
    pallas_call x1, Pallas kernels, on_device(): call(load_kernel, pair_count, [hbm] * 6, [row_out] * 4 + [(pl.BlockSpec((...  1.79 us
    pallas_call x1, Pallas kernels, band(): call(own_keys_kernel, pair_count, [row_spec, row_spec, own_sq, own_sq, ro...  1.64 us
    pallas_call x1, Pallas kernels, band(): call(grads_kernel, pair_count, [row_spec] * 3 + [keyt_spec, delta_spec, h...  1.38 us
    pallas_call x1, Pallas kernels, band(): call(probs_kernel, pair_count, [row_spec, row_spec, low_spec, stat_spec,...  1.33 us
    pallas_call x1, Pallas kernels, band(): call(finish_kernel, pair_count, [row_spec, ridden_spec] + [gain_spec] * l...  0.75 us
  transfers between devices with their start and end apart: 6, of which 2 were waited for; matrix products, arithmetic and copies ran while one was open for 0% of the time, Pallas kernels for 30%

profile of v3, /device:TPU:0, one launch (start us, length us, event | category | flops | bytes accessed | tf_op | source)
XLA Modules:
  0.0 22.1 jit_solution(8396922254549365575)
XLA Ops:
  0.6 1.8 %shard_map.102 = (bf16[1,1024,128]{2,1,0:T(8,128)(2,1)S(1)}, bf16[1,1024,128]{2,1,0:T(8,128)(2,1)S(1)}, bf16[1,1024,128]{2,1,0:T(8,128)(2,1)S(1)}, bf16[1,1024,1...) custom-call(s32[1,4096]{1,0:T(1,128)} %doc_hbm.1, s32[1,4096]{1,0:T(1,128)} %win_hbm.1, ...), custom_call_target="tpu_custom_call" | custom-call | flops 1 | bytes 1 | tf_op jit(solution)/shard_map/pallas_call | solution.py:342
  3.1 19.0 %conditional.1 = (bf16[1,1024,128]{2,1,0:T(8,128)(2,1)}, bf16[1,1024,128]{2,1,0:T(8,128)(2,1)}, bf16[1,1024,128]{2,1,0:T(8,128)(2,1)}, f32[1,1,128]{2,1,0:T(1,128)}) conditional(s32[]{:T(128)} %bitcast, (bf16[1,1024,128]{2,1,0:T(8,128)(2,1)S(1)}, bf16[1,1024,128]{2,1,0:T(8,128)(2,1)S(1)}, ...), branch_computations={%region_0.0_spmd, %region_1.0_spmd, %region_2.0_spmd, %region_3.0_... | conditional | flops 11000000512 | bytes 4610353 | solution.py:354
  3.1 3.0 %collective-permute-start = (bf16[1,384,128]{2,1,0:T(8,128)(2,1)S(1)}, bf16[1,384,128]{2,1,0:T(8,128)(2,1)S(1)}, u32[]{:S(2)}, u32[]{:S(2)}) collective-permute-start(bf16[1,384,128]{2,1,0:T(8,128)(2,1)S(1)} %slice.20), channel_id=1, source_target_pairs={{0,8},{8,16},{16,24},{24,0},{1,9},{9,17},{17,25},{25,1},{2,10},{10... | collective-permute-start | bytes 294920 | tf_op jit(solution)/shard_map/cond/branch_0_fun/ppermute | solution.py:27
  6.1 1.5 %collective-permute-start.1 = (bf16[1,384,128]{2,1,0:T(8,128)(2,1)S(1)}, bf16[1,384,128]{2,1,0:T(8,128)(2,1)S(1)}, u32[]{:S(2)}, u32[]{:S(2)}) collective-permute-start(bf16[1,384,128]{2,1,0:T(8,128)(2,1)S(1)} %slice.21), channel_id=1, source_target_pairs={{0,8},{8,16},{16,24},{24,0},{1,9},{9,17},{17,25},{25,1},{2,10},{10... | collective-permute-start | bytes 294920 | tf_op jit(solution)/shard_map/cond/branch_0_fun/ppermute | solution.py:27
  7.7 2.3 %branch_0_fun.5 = (bf16[1,1024,128]{2,1,0:T(8,128)(2,1)S(1)}, bf16[1,128,1024]{2,1,0:T(8,128)(2,1)S(1)}, f32[1,8,1024]{2,1,0:T(8,128)S(1)}, f32[1,1024,1024]{2,1,0:T(8,128)S(1)}, f32[1,1024,1024]{2,1,0:T(8,128)S(1)}) custom-call(bf16[1,1024,128]{2,1,0:T(8,128)(2,1)S(1)} %get-tuple-element.61.q_ref, bf16[1,1024,128]{2,1,0:T(8,128)(2,1)S(1)} %get-tuple-element.62.k_ref, ...), custom_call_target="tpu_custom_call" | custom-call | flops 1 | bytes 1 | tf_op jit(solution)/shard_map/cond/branch_0_fun/pallas_call | solution.py:253
  9.9 0.7 %collective-permute-done.kh_ref = bf16[1,384,128]{2,1,0:T(8,128)(2,1)S(1)} collective-permute-done((bf16[1,384,128]{2,1,0:T(8,128)(2,1)S(1)}, bf16[1,384,128]{2,1,0:T(8,128)(2,1)S(1)}, u32[]{:S(2)}, u32[]{:S(2)}) %collective-permute-start) | collective-permute-done | bytes 98336 | tf_op jit(solution)/shard_map/cond/branch_0_fun/ppermute | solution.py:27
  10.6 1.3 %branch_0_fun.6 = (f32[1,1,1024]{2,1,0:T(1,128)S(1)}, bf16[1,384,1024]{2,1,0:T(8,128)(2,1)S(1)}, bf16[1,1024,1024]{2,1,0:T(8,128)(2,1)S(1)}, bf16[1,384,128]{2,1,0:T(8,128)(2,1)S(1)}) custom-call(bf16[1,1024,128]{2,1,0:T(8,128)(2,1)S(1)} %get-tuple-element.66.scaled_ref, bf16[1,1024,128]{2,1,0:T(8,128)(2,1)S(1)} %get-tuple-element.60.g_ref, ...), custom_call_target="tpu_custom_call" | custom-call | flops 1 | bytes 1 | tf_op jit(solution)/shard_map/cond/branch_0_fun/pallas_call | solution.py:268
  11.9 2.1 %collective-permute-start.2 = (bf16[1,384,128]{2,1,0:T(8,128)(2,1)S(1)}, bf16[1,384,128]{2,1,0:T(8,128)(2,1)S(1)}, u32[]{:S(2)}, u32[]{:S(2)}) collective-permute-start(bf16[1,384,128]{2,1,0:T(8,128)(2,1)S(1)} %get-tuple-element.76), channel_id=1, source_target_pairs={{0,24},{8,0},{16,8},{24,16},{1,25},{9,1},{17,9},{25,17},{2,26},{10... | collective-permute-start | bytes 294920 | tf_op jit(solution)/shard_map/cond/branch_0_fun/ppermute | solution.py:27
  14.0 0.0 collective-permute-done.1.vh_ref
  14.0 0.0 copy-start
  14.1 1.4 %branch_0_fun.7 = (f32[1,1024,128]{2,1,0:T(8,128)S(1)}, bf16[1,400,128]{2,1,0:T(8,128)(2,1)S(1)}, f32[1,1,128]{2,1,0:T(1,128)S(1)}, bf16[1,1024,1024]{2,1,0:T(8,128)(2,1)S(1)}) custom-call(bf16[1,1024,128]{2,1,0:T(8,128)(2,1)S(1)} %get-tuple-element.61.q_ref, bf16[1,1024,128]{2,1,0:T(8,128)(2,1)S(1)} %get-tuple-element.66.scaled_ref, ...), custom_call_target="tpu_custom_call" | custom-call | flops 10000000000 | bytes 1 | tf_op jit(solution)/shard_map/cond/branch_0_fun/pallas_call | solution.py:283
  15.4 1.4 %collective-permute-start.3 = (bf16[1,400,128]{2,1,0:T(8,128)(2,1)S(1)}, bf16[1,400,128]{2,1,0:T(8,128)(2,1)S(1)}, u32[]{:S(2)}, u32[]{:S(2)}) collective-permute-start(bf16[1,400,128]{2,1,0:T(8,128)(2,1)S(1)} %get-tuple-element.79), channel_id=1, source_target_pairs={{0,24},{8,0},{16,8},{24,16},{1,25},{9,1},{17,9},{25,17},{2,26},{10... | collective-permute-start | bytes 307208 | tf_op jit(solution)/shard_map/cond/branch_0_fun/ppermute | solution.py:27
  16.9 0.7 %collective-permute-start.4 = (f32[1,1,128]{2,1,0:T(1,128)S(1)}, f32[1,1,128]{2,1,0:T(1,128)S(1)}, u32[]{:S(2)}, u32[]{:S(2)}) collective-permute-start(f32[1,1,128]{2,1,0:T(1,128)S(1)} %get-tuple-element.80.refs_0_), channel_id=1, source_target_pairs={{0,8},{8,16},{16,24},{24,0},{1,9},{9,17},{17,25},{25,1},{2,10},{10... | collective-permute-start | bytes 1544 | tf_op jit(solution)/shard_map/cond/branch_0_fun/ppermute | solution.py:27
  17.5 0.5 %collective-permute-start.5 = (f32[1,1,128]{2,1,0:T(1,128)S(1)}, f32[1,1,128]{2,1,0:T(1,128)S(1)}, u32[]{:S(2)}, u32[]{:S(2)}) collective-permute-start(f32[1,1,128]{2,1,0:T(1,128)S(1)} %get-tuple-element.80.refs_0_), channel_id=1, source_target_pairs={{0,16},{8,24},{16,0},{24,8},{1,17},{9,25},{17,1},{25,9},{2,18},{10... | collective-permute-start | bytes 1544 | tf_op jit(solution)/shard_map/cond/branch_0_fun/ppermute | solution.py:27
  18.0 0.0 collective-permute-done.2.back_ref
  18.0 0.0 copy-done
  18.0 1.6 %branch_0_fun.8 = (bf16[1,1024,128]{2,1,0:T(8,128)(2,1)}, bf16[1,1024,128]{2,1,0:T(8,128)(2,1)}, f32[1,1024,128]{2,1,0:T(8,128)S(1)}) custom-call(bf16[1,1024,128]{2,1,0:T(8,128)(2,1)S(1)} %get-tuple-element.60.g_ref, bf16[1,1024,128]{2,1,0:T(8,128)(2,1)S(1)} %get-tuple-element.66.scaled_ref, bf16[1,1024,1024]{2,1,0:T(8,128)(2,1)S(1)} %get-tuple-element.69.probs_ref, ...), custom_call_target="tpu_custom_call" | custom-call | flops 1000000000 | bytes 1 | tf_op jit(solution)/shard_map/cond/branch_0_fun/pallas_call | solution.py:309
  19.6 1.7 %collective-permute-done.4.refs_1_ = f32[1,1,128]{2,1,0:T(1,128)S(1)} collective-permute-done((f32[1,1,128]{2,1,0:T(1,128)S(1)}, f32[1,1,128]{2,1,0:T(1,128)S(1)}, u32[]{:S(2)}, u32[]{:S(2)}) %collective-permute-start.4) | collective-permute-done | bytes 544 | tf_op jit(solution)/shard_map/cond/branch_0_fun/ppermute | solution.py:27
  21.3 0.0 collective-permute-done.5.refs_2_
  21.3 0.0 collective-permute-done.3.back_ref
  21.3 0.7 %branch_0_fun.9 = (bf16[1,1024,128]{2,1,0:T(8,128)(2,1)}, f32[1,1,128]{2,1,0:T(1,128)}) custom-call(f32[1,1024,128]{2,1,0:T(8,128)S(1)} %get-tuple-element.78.own_ref, bf16[1,400,128]{2,1,0:T(8,128)(2,1)S(1)} %collective-permute-done.3.back_ref, f32[1,1,128]{2,1,0:T(1,128)S(1)} %get-tuple-element.80.refs_0_, ...), custom_call_target="tpu_custom_call" | custom-call | flops 1 | bytes 1 | tf_op jit(solution)/shard_map/cond/branch_0_fun/pallas_call | solution.py:317
  (2 shorter events, 0.0 us)
Async XLA Ops:
  3.1 7.4 %collective-permute-start = (bf16[1,384,128]{2,1,0:T(8,128)(2,1)S(1)}, bf16[1,384,128]{2,1,0:T(8,128)(2,1)S(1)}, u32[]{:S(2)}, u32[]{:S(2)}) collective-permute-start(bf16[1,384,128]{2,1,0:T(8,128)(2,1)S(1)} %slice.20), channel_id=1, source_target_pairs={{0,8},{8,16},{16,24},{24,0},{1,9},{9,17},{17,25},{25,1},{2,10},{10... | collective-permute-start | bytes 294920 | tf_op jit(solution)/shard_map/cond/branch_0_fun/ppermute | solution.py:27
  6.1 7.9 %collective-permute-start.1 = (bf16[1,384,128]{2,1,0:T(8,128)(2,1)S(1)}, bf16[1,384,128]{2,1,0:T(8,128)(2,1)S(1)}, u32[]{:S(2)}, u32[]{:S(2)}) collective-permute-start(bf16[1,384,128]{2,1,0:T(8,128)(2,1)S(1)} %slice.21), channel_id=1, source_target_pairs={{0,8},{8,16},{16,24},{24,0},{1,9},{9,17},{17,25},{25,1},{2,10},{10... | collective-permute-start | bytes 294920 | tf_op jit(solution)/shard_map/cond/branch_0_fun/ppermute | solution.py:27
  11.9 6.1 %collective-permute-start.2 = (bf16[1,384,128]{2,1,0:T(8,128)(2,1)S(1)}, bf16[1,384,128]{2,1,0:T(8,128)(2,1)S(1)}, u32[]{:S(2)}, u32[]{:S(2)}) collective-permute-start(bf16[1,384,128]{2,1,0:T(8,128)(2,1)S(1)} %get-tuple-element.76), channel_id=1, source_target_pairs={{0,24},{8,0},{16,8},{24,16},{1,25},{9,1},{17,9},{25,17},{2,26},{10... | collective-permute-start | bytes 294920 | tf_op jit(solution)/shard_map/cond/branch_0_fun/ppermute | solution.py:27
  14.0 3.9 %copy-start = (f32[1,1,128]{2,1,0:T(1,128)S(1)}, f32[1,1,128]{2,1,0:T(1,128)}, u32[]{:S(2)}) copy-start(f32[1,1,128]{2,1,0:T(1,128)} %get-tuple-element.64.gain_ref) | copy-start | bytes 1540 | tf_op jit(solution)/shard_map/cond
  15.4 5.9 %collective-permute-start.3 = (bf16[1,400,128]{2,1,0:T(8,128)(2,1)S(1)}, bf16[1,400,128]{2,1,0:T(8,128)(2,1)S(1)}, u32[]{:S(2)}, u32[]{:S(2)}) collective-permute-start(bf16[1,400,128]{2,1,0:T(8,128)(2,1)S(1)} %get-tuple-element.79), channel_id=1, source_target_pairs={{0,24},{8,0},{16,8},{24,16},{1,25},{9,1},{17,9},{25,17},{2,26},{10... | collective-permute-start | bytes 307208 | tf_op jit(solution)/shard_map/cond/branch_0_fun/ppermute | solution.py:27
  16.9 4.4 %collective-permute-start.4 = (f32[1,1,128]{2,1,0:T(1,128)S(1)}, f32[1,1,128]{2,1,0:T(1,128)S(1)}, u32[]{:S(2)}, u32[]{:S(2)}) collective-permute-start(f32[1,1,128]{2,1,0:T(1,128)S(1)} %get-tuple-element.80.refs_0_), channel_id=1, source_target_pairs={{0,8},{8,16},{16,24},{24,0},{1,9},{9,17},{17,25},{25,1},{2,10},{10... | collective-permute-start | bytes 1544 | tf_op jit(solution)/shard_map/cond/branch_0_fun/ppermute | solution.py:27
  17.5 3.8 %collective-permute-start.5 = (f32[1,1,128]{2,1,0:T(1,128)S(1)}, f32[1,1,128]{2,1,0:T(1,128)S(1)}, u32[]{:S(2)}, u32[]{:S(2)}) collective-permute-start(f32[1,1,128]{2,1,0:T(1,128)S(1)} %get-tuple-element.80.refs_0_), channel_id=1, source_target_pairs={{0,16},{8,24},{16,0},{24,8},{1,17},{9,25},{17,1},{25,9},{2,18},{10... | collective-permute-start | bytes 1544 | tf_op jit(solution)/shard_map/cond/branch_0_fun/ppermute | solution.py:27

commit v4 on v3

--- a/solution.py
+++ b/solution.py
@@ -17,7 +17,7 @@
 NEG = -1e30
 M_ROW, L_ROW, D_ROW = 0, 1, 2
 LIGHT, HEAVY = 1, 10**10
-FEWEST = 3
+FEWEST = 4
 RIDERS = 16
 
 
@@ -89,20 +89,23 @@
     rows = q_ref.shape[1]
     keyt_ref[0] = k_ref[0].T
     scaled_ref[0] = (q_ref[0].astype(jnp.float32) * gain_ref[0]).astype(jnp.bfloat16)
-    for start, stop in groups(rows):
-        logits = mm_t(k_ref[0, :stop, :], scaled_ref[0, start:stop, :]) * factor
+
+    @pl.loop(0, rows // GROUP)
+    def _(group):
+        own = pl.ds(pl.multiple_of(group * GROUP, GROUP), GROUP)
+        logits = mm_t(k_ref[0], scaled_ref[0, own, :]) * factor
         key_at = lax.broadcasted_iota(jnp.int32, logits.shape, 0)
-        query_at = start + lax.broadcasted_iota(jnp.int32, logits.shape, 1)
-        visible = (key_at >= low_ref[:, start:stop]) & (key_at <= query_at)
+        query_at = group * GROUP + lax.broadcasted_iota(jnp.int32, (1, GROUP), 1)
+        visible = (key_at >= low_ref[:, own]) & (key_at <= query_at)
         logits = jnp.where(visible, logits, NEG)
         top = jnp.max(logits, axis=0, keepdims=True)
         weights = jnp.exp2(logits - top)
-        slopes = mm_t(v_ref[0, :stop, :], g_ref[0, start:stop, :])
-        weight_ref[0, :stop, start:stop] = weights
-        slope_ref[0, :stop, start:stop] = slopes
-        stats_ref[0, M_ROW : M_ROW + 1, start:stop] = top
-        stats_ref[0, L_ROW : L_ROW + 1, start:stop] = jnp.sum(weights, axis=0, keepdims=True)
-        stats_ref[0, D_ROW : D_ROW + 1, start:stop] = jnp.sum(weights * slopes, axis=0, keepdims=True)
+        slopes = mm_t(v_ref[0], g_ref[0, own, :])
+        weight_ref[0, :, own] = weights
+        slope_ref[0, :, own] = slopes
+        stats_ref[0, M_ROW : M_ROW + 1, own] = top
+        stats_ref[0, L_ROW : L_ROW + 1, own] = jnp.sum(weights, axis=0, keepdims=True)
+        stats_ref[0, D_ROW : D_ROW + 1, own] = jnp.sum(weights * slopes, axis=0, keepdims=True)
 
 
 def probs_kernel(
@@ -132,6 +135,8 @@
             share = 1.0 / total
         delta_ref[0, 0:1, start:stop] = part_ref[0, D_ROW : D_ROW + 1, start:stop] * share
         probs_ref[0, :stop, start:stop] = (weight_ref[0, :stop, start:stop] * share).astype(jnp.bfloat16)
+        if stop < rows:
+            probs_ref[0, stop:, start:stop] = jnp.zeros((rows - stop, stop - start), jnp.bfloat16)
     for first, last, seen in halo_chunks(halo, rows):
         dv_ref[0, first:last, :] = mm(hprobs_ref[0, first:last, :seen], g_ref[0, :seen, :]).astype(jnp.bfloat16)
 
@@ -156,6 +161,8 @@
         probs = probs_ref[0, :stop, start:stop].astype(jnp.float32)
         grads = (probs * (slope_ref[0, :stop, start:stop] - delta)).astype(jnp.bfloat16)
         grads_ref[0, :stop, start:stop] = grads
+        if stop < rows:
+            grads_ref[0, stop:, start:stop] = jnp.zeros((rows - stop, stop - start), jnp.bfloat16)
         dq = mm(keyt_ref[0, :, :stop], grads)
         if start < PREV:
             dq = dq + mm(halo_cols[:, first:], hgrads)
@@ -177,20 +184,21 @@
 
 
 def own_keys_kernel(
-    g_ref, scaled_ref, probs_ref, grads_ref, dq_ref, gain_ref, back_ref, gq_ref, dv_ref, dk_ref, *, score_scale
+    g_ref, scaled_ref, probs_ref, grads_ref, dq_ref, gain_ref, back_ref, gq_ref, dv_ref, dk_ref, dsum_ref, *, score_scale
 ):
     rows = g_ref.shape[1]
     gq_ref[0] = (dq_ref[0] * gain_ref[0]).astype(jnp.bfloat16)
     lead = rows - back_ref.shape[1]
-    for first, last in groups(rows):
-        own = mm(probs_ref[0, first:last, first:], g_ref[0, first:, :])
-        cut = min(max(lead - first, 0), last - first)
-        if cut:
-            dv_ref[0, first : first + cut, :] = own[:cut].astype(jnp.bfloat16)
-        if cut < last - first:
-            back = back_ref[0, first + cut - lead : last - lead, :].astype(jnp.float32)
-            dv_ref[0, first + cut : last, :] = (own[cut:] + back).astype(jnp.bfloat16)
-        dk_ref[0, first:last, :] = mm(grads_ref[0, first:last, first:], scaled_ref[0, first:, :]) * score_scale
+
+    @pl.loop(0, rows // GROUP)
+    def _(group):
+        own = pl.ds(pl.multiple_of(group * GROUP, GROUP), GROUP)
+        dsum_ref[own, :] = mm(probs_ref[0, own, :], g_ref[0])
+        dk_ref[0, own, :] = mm(grads_ref[0, own, :], scaled_ref[0]) * score_scale
+
+    if lead:
+        dv_ref[0, :lead, :] = dsum_ref[:lead, :].astype(jnp.bfloat16)
+    dv_ref[0, lead:, :] = (dsum_ref[lead:, :] + back_ref[0].astype(jnp.float32)).astype(jnp.bfloat16)
 
 
 def finish_kernel(own_ref, back_ref, *refs, riding):
@@ -312,6 +320,7 @@
         [row_spec, row_spec, own_sq, own_sq, row_spec, gain_spec, halo_spec],
         (row_out, row_out, wide_out),
         10**9,
+        scratch=[pltpu.VMEM((rows, width), f32)],
         score_scale=score_scale,
     )(grad_in, scaled, own_probs, own_grads, dq, gain_rows, dv_back)
     grad_keys, gain_sum = call(

time: 22.3 us -> 27.1 us (1.22)
  Pallas kernels: 9.14 us -> 13.2 us
  starting transfers between devices: 9.2 us -> 10.6 us
  waiting for transfers between devices: 2.35 us -> 1.78 us
    pallas_call x1, Pallas kernels: 2.25 us -> 4.18 us  [band(): call(own_stats_kernel, pair_count, [row_spec] * 4 + [gain_spec, low_spec]...]
    ppermute x6, starting transfers between devices: 9.2 us -> 10.6 us  [shift(): return lax.ppermute(value, axis, pairs)]
    pallas_call x1, Pallas kernels: 1.64 us -> 2.47 us  [band(): call(own_keys_kernel, pair_count, [row_spec, row_spec, own_sq, own_sq, ro...]
    pallas_call x1, Pallas kernels: 1.38 us -> 2.1 us  [band(): call(grads_kernel, pair_count, [row_spec] * 3 + [keyt_spec, delta_spec, h...]
    ppermute x6, waiting for transfers between devices: 2.35 us -> 1.78 us  [shift(): return lax.ppermute(value, axis, pairs)]
    pallas_call x1, Pallas kernels: 1.33 us -> 1.85 us  [band(): call(probs_kernel, pair_count, [row_spec, row_spec, low_spec, stat_spec,...]
  transfers between devices with their start and end apart: 6 -> 6, of which waited for: 2 -> 2; matrix products, arithmetic and copies ran while one was open for 0% -> 0% of each run, Pallas kernels for 30% -> 39%
where the time goes in v4:
time: 27.1 us; the launch traced here: 26.9 us
  Pallas kernels  13.2 us (49%)
  starting transfers between devices  10.6 us (39%)
  waiting for transfers between devices  1.78 us (7%)
  between operations  1.29 us (5%)
    ppermute x6, starting transfers between devices, shift(): return lax.ppermute(value, axis, pairs)  10.6 us
    pallas_call x1, Pallas kernels, band(): call(own_stats_kernel, pair_count, [row_spec] * 4 + [gain_spec, low_spec]...  4.18 us
    pallas_call x1, Pallas kernels, band(): call(own_keys_kernel, pair_count, [row_spec, row_spec, own_sq, own_sq, ro...  2.47 us
    pallas_call x1, Pallas kernels, band(): call(grads_kernel, pair_count, [row_spec] * 3 + [keyt_spec, delta_spec, h...  2.1 us
    pallas_call x1, Pallas kernels, band(): call(probs_kernel, pair_count, [row_spec, row_spec, low_spec, stat_spec,...  1.85 us
    pallas_call x1, Pallas kernels, on_device(): call(load_kernel, pair_count, [hbm] * 6, [row_out] * 4 + [(pl.BlockSpec((...  1.79 us
    ppermute x6, waiting for transfers between devices, shift(): return lax.ppermute(value, axis, pairs)  1.78 us
    pallas_call x1, Pallas kernels, band(): call(finish_kernel, pair_count, [row_spec, ridden_spec] + [gain_spec] * l...  0.76 us
  transfers between devices with their start and end apart: 6, of which 2 were waited for; matrix products, arithmetic and copies ran while one was open for 0% of the time, Pallas kernels for 39%

profile of v4, /device:TPU:0, one launch (start us, length us, event | category | flops | bytes accessed | tf_op | source)
XLA Modules:
  0.0 26.9 jit_solution(11332987452724641061)
XLA Ops:
  0.6 1.8 %shard_map.102 = (bf16[1,1024,128]{2,1,0:T(8,128)(2,1)S(1)}, bf16[1,1024,128]{2,1,0:T(8,128)(2,1)S(1)}, bf16[1,1024,128]{2,1,0:T(8,128)(2,1)S(1)}, bf16[1,1024,1...) custom-call(s32[1,4096]{1,0:T(1,128)} %doc_hbm.1, s32[1,4096]{1,0:T(1,128)} %win_hbm.1, ...), custom_call_target="tpu_custom_call" | custom-call | flops 1 | bytes 1 | tf_op jit(solution)/shard_map/pallas_call | solution.py:351
  3.1 23.8 %conditional.1 = (bf16[1,1024,128]{2,1,0:T(8,128)(2,1)}, bf16[1,1024,128]{2,1,0:T(8,128)(2,1)}, bf16[1,1024,128]{2,1,0:T(8,128)(2,1)}, f32[1,1,128]{2,1,0:T(1,128)}) conditional(s32[]{:T(128)} %bitcast, (bf16[1,1024,128]{2,1,0:T(8,128)(2,1)S(1)}, bf16[1,1024,128]{2,1,0:T(8,128)(2,1)S(1)}, ...), branch_computations={%region_0.0_spmd, %region_1.0_spmd, %region_2.0_spmd, %region_3.0_... | conditional | flops 11000000512 | bytes 4610353 | solution.py:363
  3.1 3.0 %collective-permute-start.12 = (bf16[1,768,128]{2,1,0:T(8,128)(2,1)S(1)}, bf16[1,768,128]{2,1,0:T(8,128)(2,1)S(1)}, u32[]{:S(2)}, u32[]{:S(2)}) collective-permute-start(bf16[1,768,128]{2,1,0:T(8,128)(2,1)S(1)} %slice.20), channel_id=1, source_target_pairs={{0,8},{8,16},{16,24},{24,0},{1,9},{9,17},{17,25},{25,1},{2,10},{10... | collective-permute-start | bytes 589832 | tf_op jit(solution)/shard_map/cond/branch_2_fun/ppermute | solution.py:27
  6.1 1.7 %collective-permute-start.13 = (bf16[1,768,128]{2,1,0:T(8,128)(2,1)S(1)}, bf16[1,768,128]{2,1,0:T(8,128)(2,1)S(1)}, u32[]{:S(2)}, u32[]{:S(2)}) collective-permute-start(bf16[1,768,128]{2,1,0:T(8,128)(2,1)S(1)} %slice.21), channel_id=1, source_target_pairs={{0,8},{8,16},{16,24},{24,0},{1,9},{9,17},{17,25},{25,1},{2,10},{10... | collective-permute-start | bytes 589832 | tf_op jit(solution)/shard_map/cond/branch_2_fun/ppermute | solution.py:27
  7.9 4.2 %branch_2_fun.5 = (bf16[1,1024,128]{2,1,0:T(8,128)(2,1)S(1)}, bf16[1,128,1024]{2,1,0:T(8,128)(2,1)S(1)}, f32[1,8,1024]{2,1,0:T(8,128)S(1)}, f32[1,1024,1024]{2,1,0:T(8,128)S(1)}, f32[1,1024,1024]{2,1,0:T(8,128)S(1)}) custom-call(bf16[1,1024,128]{2,1,0:T(8,128)(2,1)S(1)} %get-tuple-element.97.q_ref, bf16[1,1024,128]{2,1,0:T(8,128)(2,1)S(1)} %get-tuple-element.98.k_ref, ...), custom_call_target="tpu_custom_call" | custom-call | flops 1 | bytes 1 | tf_op jit(solution)/shard_map/cond/branch_2_fun/pallas_call | solution.py:261
  12.0 0.8 %collective-permute-done.12.kh_ref = bf16[1,768,128]{2,1,0:T(8,128)(2,1)S(1)} collective-permute-done((bf16[1,768,128]{2,1,0:T(8,128)(2,1)S(1)}, bf16[1,768,128]{2,1,0:T(8,128)(2,1)S(1)}, u32[]{:S(2)}, u32[]{:S(2)}) %collective-permute-start.12) | collective-permute-done | bytes 196640 | tf_op jit(solution)/shard_map/cond/branch_2_fun/ppermute | solution.py:27
  12.8 1.9 %branch_2_fun.6 = (f32[1,1,1024]{2,1,0:T(1,128)S(1)}, bf16[1,768,1024]{2,1,0:T(8,128)(2,1)S(1)}, bf16[1,1024,1024]{2,1,0:T(8,128)(2,1)S(1)}, bf16[1,768,128]{2,1,0:T(8,128)(2,1)S(1)}) custom-call(bf16[1,1024,128]{2,1,0:T(8,128)(2,1)S(1)} %get-tuple-element.102.scaled_ref, bf16[1,1024,128]{2,1,0:T(8,128)(2,1)S(1)} %get-tuple-element.96.g_ref, ...), custom_call_target="tpu_custom_call" | custom-call | flops 1 | bytes 1 | tf_op jit(solution)/shard_map/cond/branch_2_fun/pallas_call | solution.py:276
  14.7 2.1 %collective-permute-start.14 = (bf16[1,768,128]{2,1,0:T(8,128)(2,1)S(1)}, bf16[1,768,128]{2,1,0:T(8,128)(2,1)S(1)}, u32[]{:S(2)}, u32[]{:S(2)}) collective-permute-start(bf16[1,768,128]{2,1,0:T(8,128)(2,1)S(1)} %get-tuple-element.112), channel_id=1, source_target_pairs={{0,24},{8,0},{16,8},{24,16},{1,25},{9,1},{17,9},{25,17},{2,26},{10... | collective-permute-start | bytes 589832 | tf_op jit(solution)/shard_map/cond/branch_2_fun/ppermute | solution.py:27
  16.8 0.0 collective-permute-done.13.vh_ref
  16.8 0.0 copy-start.2
  16.8 2.1 %branch_2_fun.7 = (f32[1,1024,128]{2,1,0:T(8,128)S(1)}, bf16[1,784,128]{2,1,0:T(8,128)(2,1)S(1)}, f32[1,1,128]{2,1,0:T(1,128)S(1)}, bf16[1,1024,1024]{2,1,0:T(8,128)(2,1)S(1)}) custom-call(bf16[1,1024,128]{2,1,0:T(8,128)(2,1)S(1)} %get-tuple-element.97.q_ref, bf16[1,1024,128]{2,1,0:T(8,128)(2,1)S(1)} %get-tuple-element.102.scaled_ref, ...), custom_call_target="tpu_custom_call" | custom-call | flops 10000000000 | bytes 1 | tf_op jit(solution)/shard_map/cond/branch_2_fun/pallas_call | solution.py:291
  18.9 1.5 %collective-permute-start.15 = (bf16[1,784,128]{2,1,0:T(8,128)(2,1)S(1)}, bf16[1,784,128]{2,1,0:T(8,128)(2,1)S(1)}, u32[]{:S(2)}, u32[]{:S(2)}) collective-permute-start(bf16[1,784,128]{2,1,0:T(8,128)(2,1)S(1)} %get-tuple-element.115), channel_id=1, source_target_pairs={{0,24},{8,0},{16,8},{24,16},{1,25},{9,1},{17,9},{25,17},{2,26},{10... | collective-permute-start | bytes 602120 | tf_op jit(solution)/shard_map/cond/branch_2_fun/ppermute | solution.py:27
  20.4 0.6 %collective-permute-start.16 = (f32[1,1,128]{2,1,0:T(1,128)S(1)}, f32[1,1,128]{2,1,0:T(1,128)S(1)}, u32[]{:S(2)}, u32[]{:S(2)}) collective-permute-start(f32[1,1,128]{2,1,0:T(1,128)S(1)} %get-tuple-element.116.refs_0_), channel_id=1, source_target_pairs={{0,8},{8,16},{16,24},{24,0},{1,9},{9,17},{17,25},{25,1},{2,10},{10... | collective-permute-start | bytes 1544 | tf_op jit(solution)/shard_map/cond/branch_2_fun/ppermute | solution.py:27
  21.0 1.7 %collective-permute-start.17 = (f32[1,1,128]{2,1,0:T(1,128)S(1)}, f32[1,1,128]{2,1,0:T(1,128)S(1)}, u32[]{:S(2)}, u32[]{:S(2)}) collective-permute-start(f32[1,1,128]{2,1,0:T(1,128)S(1)} %get-tuple-element.116.refs_0_), channel_id=1, source_target_pairs={{0,16},{8,24},{16,0},{24,8},{1,17},{9,25},{17,1},{25,9},{2,18},{10... | collective-permute-start | bytes 1544 | tf_op jit(solution)/shard_map/cond/branch_2_fun/ppermute | solution.py:27
  22.6 0.0 collective-permute-done.14.back_ref
  22.6 0.0 copy-done.2
  22.6 2.5 %branch_2_fun.8 = (bf16[1,1024,128]{2,1,0:T(8,128)(2,1)}, bf16[1,1024,128]{2,1,0:T(8,128)(2,1)}, f32[1,1024,128]{2,1,0:T(8,128)S(1)}) custom-call(bf16[1,1024,128]{2,1,0:T(8,128)(2,1)S(1)} %get-tuple-element.96.g_ref, bf16[1,1024,128]{2,1,0:T(8,128)(2,1)S(1)} %get-tuple-element.102.scaled_ref, bf16[1,1024,1024]{2,1,0:T(8,128)(2,1)S(1)} %get-tuple-element.105.probs_ref, ...), custom_call_target="tpu_custom_call" | custom-call | flops 1000000000 | bytes 1 | tf_op jit(solution)/shard_map/cond/branch_2_fun/pallas_call | solution.py:317
  25.1 1.0 %collective-permute-done.16.refs_1_ = f32[1,1,128]{2,1,0:T(1,128)S(1)} collective-permute-done((f32[1,1,128]{2,1,0:T(1,128)S(1)}, f32[1,1,128]{2,1,0:T(1,128)S(1)}, u32[]{:S(2)}, u32[]{:S(2)}) %collective-permute-start.16) | collective-permute-done | bytes 544 | tf_op jit(solution)/shard_map/cond/branch_2_fun/ppermute | solution.py:27
  26.1 0.0 collective-permute-done.17.refs_2_
  26.1 0.0 collective-permute-done.15.back_ref
  26.1 0.8 %branch_2_fun.9 = (bf16[1,1024,128]{2,1,0:T(8,128)(2,1)}, f32[1,1,128]{2,1,0:T(1,128)}) custom-call(f32[1,1024,128]{2,1,0:T(8,128)S(1)} %get-tuple-element.114.own_ref, bf16[1,784,128]{2,1,0:T(8,128)(2,1)S(1)} %collective-permute-done.15.back_ref, f32[1,1,128]{2,1,0:T(1,128)S(1)} %get-tuple-element.116.refs_0_, ...), custom_call_target="tpu_custom_call" | custom-call | flops 1 | bytes 1 | tf_op jit(solution)/shard_map/cond/branch_2_fun/pallas_call | solution.py:326
  (2 shorter events, 0.0 us)
Async XLA Ops:
  3.1 9.7 %collective-permute-start.12 = (bf16[1,768,128]{2,1,0:T(8,128)(2,1)S(1)}, bf16[1,768,128]{2,1,0:T(8,128)(2,1)S(1)}, u32[]{:S(2)}, u32[]{:S(2)}) collective-permute-start(bf16[1,768,128]{2,1,0:T(8,128)(2,1)S(1)} %slice.20), channel_id=1, source_target_pairs={{0,8},{8,16},{16,24},{24,0},{1,9},{9,17},{17,25},{25,1},{2,10},{10... | collective-permute-start | bytes 589832 | tf_op jit(solution)/shard_map/cond/branch_2_fun/ppermute | solution.py:27
  6.1 10.6 %collective-permute-start.13 = (bf16[1,768,128]{2,1,0:T(8,128)(2,1)S(1)}, bf16[1,768,128]{2,1,0:T(8,128)(2,1)S(1)}, u32[]{:S(2)}, u32[]{:S(2)}) collective-permute-start(bf16[1,768,128]{2,1,0:T(8,128)(2,1)S(1)} %slice.21), channel_id=1, source_target_pairs={{0,8},{8,16},{16,24},{24,0},{1,9},{9,17},{17,25},{25,1},{2,10},{10... | collective-permute-start | bytes 589832 | tf_op jit(solution)/shard_map/cond/branch_2_fun/ppermute | solution.py:27
  14.7 8.0 %collective-permute-start.14 = (bf16[1,768,128]{2,1,0:T(8,128)(2,1)S(1)}, bf16[1,768,128]{2,1,0:T(8,128)(2,1)S(1)}, u32[]{:S(2)}, u32[]{:S(2)}) collective-permute-start(bf16[1,768,128]{2,1,0:T(8,128)(2,1)S(1)} %get-tuple-element.112), channel_id=1, source_target_pairs={{0,24},{8,0},{16,8},{24,16},{1,25},{9,1},{17,9},{25,17},{2,26},{10... | collective-permute-start | bytes 589832 | tf_op jit(solution)/shard_map/cond/branch_2_fun/ppermute | solution.py:27
  16.8 5.9 %copy-start.2 = (f32[1,1,128]{2,1,0:T(1,128)S(1)}, f32[1,1,128]{2,1,0:T(1,128)}, u32[]{:S(2)}) copy-start(f32[1,1,128]{2,1,0:T(1,128)} %get-tuple-element.100.gain_ref) | copy-start | bytes 1540 | tf_op jit(solution)/shard_map/cond
  18.9 7.3 %collective-permute-start.15 = (bf16[1,784,128]{2,1,0:T(8,128)(2,1)S(1)}, bf16[1,784,128]{2,1,0:T(8,128)(2,1)S(1)}, u32[]{:S(2)}, u32[]{:S(2)}) collective-permute-start(bf16[1,784,128]{2,1,0:T(8,128)(2,1)S(1)} %get-tuple-element.115), channel_id=1, source_target_pairs={{0,24},{8,0},{16,8},{24,16},{1,25},{9,1},{17,9},{25,17},{2,26},{10... | collective-permute-start | bytes 602120 | tf_op jit(solution)/shard_map/cond/branch_2_fun/ppermute | solution.py:27
  20.4 5.8 %collective-permute-start.16 = (f32[1,1,128]{2,1,0:T(1,128)S(1)}, f32[1,1,128]{2,1,0:T(1,128)S(1)}, u32[]{:S(2)}, u32[]{:S(2)}) collective-permute-start(f32[1,1,128]{2,1,0:T(1,128)S(1)} %get-tuple-element.116.refs_0_), channel_id=1, source_target_pairs={{0,8},{8,16},{16,24},{24,0},{1,9},{9,17},{17,25},{25,1},{2,10},{10... | collective-permute-start | bytes 1544 | tf_op jit(solution)/shard_map/cond/branch_2_fun/ppermute | solution.py:27
  21.0 5.2 %collective-permute-start.17 = (f32[1,1,128]{2,1,0:T(1,128)S(1)}, f32[1,1,128]{2,1,0:T(1,128)S(1)}, u32[]{:S(2)}, u32[]{:S(2)}) collective-permute-start(f32[1,1,128]{2,1,0:T(1,128)S(1)} %get-tuple-element.116.refs_0_), channel_id=1, source_target_pairs={{0,16},{8,24},{16,0},{24,8},{1,17},{9,25},{17,1},{25,9},{2,18},{10... | collective-permute-start | bytes 1544 | tf_op jit(solution)/shard_map/cond/branch_2_fun/ppermute | solution.py:27
